TPU v7x, 256 devices: a whole 4x4x8 slice. The times are simulated.
256 devices in a mesh: teacher: 4 (over y), group: 8 (over z_lo, core), dp: 8 (over x, z_hi).
Axes of the slice: x: 4, y: 4, z: 8 (z_hi: 2, z_lo: 4; z = z_hi * 4 + z_lo), core: 2. Of those that a mesh axis runs over, the one named last changes fastest.
Arguments:
- teacher_feats: bfloat16 [32, 256, 4096], P('teacher', ('group', 'dp')), may hold values from -6 to 6
- student_feats: bfloat16 [8, 4, 8, 2, 256, 768], P('group', 'teacher', 'dp'), may hold values from -6 to 6
- norm_gain: float32 [8, 768], P('group'), may hold values from 0.25 to 1.75
- head_weight: bfloat16 [8, 4096, 768], P('group', ('teacher', 'dp')), may hold values from -0.21875 to 0.21875
- slot_image: int32 [8, 4, 8, 2], P(None, 'teacher'), may hold values from 0 to 7, as said below
- slot_count: int32 [8, 4, 8], P(None, 'teacher'), may hold values from 0 to 2, as said below
Outputs:
- loss: float32 [8], P('group')
- student_grad: bfloat16 [8, 4, 8, 2, 256, 768], P('group', 'teacher', 'dp')
- head_grad: float32 [8, 4096, 768], P('group', ('teacher', 'dp'))
- gain_grad: float32 [8, 768], P('group')
Inputs may be any that keep to these rules, and one draw needn't show every extreme that they name: `slot_count`: for each student and teacher batch, the counts of the 8 devices sum to 8; one device holds exactly 2 and another none. `slot_image`: for each student and teacher batch, the used slots of the devices in device order list each of the batch's 8 images once; unused slots hold image numbers to be ignored.
All inputs are finite; a program needn't handle non-finite values.
Results may differ from a plain program's by a relative error of at most 0.017.
Values may be sent and summed in bfloat16 or wider, within the bound.
A program may use at most 128 MiB of HBM per device.

v0:
```python
import jax
import jax.numpy as jnp
from jax import lax
from jax.sharding import PartitionSpec as P


def normalize(values, gain):
    center = values - jnp.mean(values, axis=-1, keepdims=True)
    spread = jnp.mean(center * center, axis=-1, keepdims=True)
    return center * lax.rsqrt(spread + 1e-06) * gain


def token_terms(logits, target, weight):
    target32 = target.astype(jnp.float32)
    inner_sum = jnp.mean(logits * target32, axis=-1)
    logit_sq = jnp.mean(logits * logits, axis=-1)
    target_sq = jnp.mean(target32 * target32, axis=-1)
    cosine = inner_sum * lax.rsqrt(logit_sq + 1e-06) * lax.rsqrt(target_sq + 1e-06)
    return jnp.sum(weight * (1.0 - cosine))


def shards(teacher_feats, student_feats, norm_gain, head_weight, slot_image, slot_count):
    groups = lax.axis_size("group")
    lanes = lax.axis_size("dp")
    group_pos = lax.axis_index("group")
    lane_pos = lax.axis_index("dp")
    slots = slot_image.shape[3]
    sliver = teacher_feats.shape[1]
    feat = teacher_feats.shape[2]
    width = student_feats.shape[5]
    patches = groups * lanes * sliver
    row_total = slots * patches
    total = teacher_feats.shape[0] * lax.axis_size("teacher") * patches
    scale = feat / 16.0
    outgoing = teacher_feats[slot_image.reshape(-1)]
    direct = outgoing.reshape(groups * lanes, slots, sliver, feat)
    arrived = lax.all_to_all(direct, ("group", "dp"), split_axis=0, concat_axis=2, tiled=True)
    target = arrived.reshape(row_total, feat)
    count_here = slot_count[group_pos, 0, lane_pos]
    used = (jnp.arange(slots, dtype=jnp.int32) < count_here).astype(jnp.float32)
    weight = jnp.repeat(used, patches)
    gain = norm_gain[0]
    values = student_feats.reshape(row_total, width).astype(jnp.float32)
    normed, pullback = jax.vjp(normalize, values, gain)
    normed_b = normed.astype(jnp.bfloat16)
    whole_head = lax.all_gather(head_weight, ("teacher", "dp"), axis=1, tiled=True)[0]
    logits = lax.dot_general(
        normed_b, whole_head, (((1,), (1,)), ((), ())), preferred_element_type=jnp.float32
    )
    loss_local = token_terms(logits, target, weight) / total
    dlogits = jax.grad(lambda inside: scale * token_terms(inside, target, weight))(logits).astype(
        jnp.bfloat16
    )
    dnormed = jnp.dot(dlogits, whole_head, preferred_element_type=jnp.float32)
    head_share = lax.psum_scatter(
        lax.dot_general(
            dlogits, normed_b, (((0,), (0,)), ((), ())), preferred_element_type=jnp.float32
        ).astype(jnp.bfloat16),
        ("teacher", "dp"),
        scatter_dimension=0,
        tiled=True,
    ).astype(jnp.float32)
    grad_values, grad_gain = pullback(dnormed)
    loss_sum, gain_sum = lax.psum((loss_local, grad_gain), ("teacher", "dp"))
    return (
        loss_sum.reshape(1),
        grad_values.astype(jnp.bfloat16).reshape(student_feats.shape),
        head_share.reshape(1, head_weight.shape[1], width),
        gain_sum.reshape(1, width),
    )


def solution(mesh):
    return jax.shard_map(
        shards,
        mesh=mesh,
        in_specs=(
            P("teacher", ("group", "dp"), None),
            P("group", "teacher", "dp", None, None, None),
            P("group", None),
            P("group", ("teacher", "dp"), None),
            P(None, "teacher", None, None),
            P(None, "teacher", None),
        ),
        out_specs=(
            P("group"),
            P("group", "teacher", "dp", None, None, None),
            P("group", ("teacher", "dp"), None),
            P("group", None),
        ),
        check_vma=False,
    )
```

profile of v0, /device:TPU:1, one launch (start us, length us, event | category | flops | bytes accessed | tf_op | source)
XLA Modules:
  0.0 506.1 jit_solution(4001634660603832901)
XLA Ops:
  7.2 0.0 copy-start
  7.2 0.0 all-gather.2.cloned.1.call-start
  7.2 0.7 all-gather.2.cloned.1.call-update
  7.9 0.8 copy.19
  8.7 0.1 reshape.153
  8.9 0.0 copy-done
  8.9 7.5 %gather_fusion = bf16[128,4,4096]{2,1,0:T(4,128)(2,1)} fusion(bf16[8,4,4096]{2,1,0:T(4,128)(2,1)S(1)} %copy-done, s32[1024]{0:T(1024)S(1)} %pad_clamp_fusion), kind=kCustom, calls=%fused_computation | custom fusion | bytes 8389120 | tf_op jit(solution)/shard_map/gather | solution.py:35
  16.4 0.0 copy-start.1
  16.4 0.0 copy-start.3
  16.4 13.3 %all-to-all-start = ((bf16[64,2,4,4096]{3,2,1,0:T(4,128)(2,1)}), bf16[64,2,4,4096]{3,2,1,0:T(4,128)(2,1)}, u32[]{:S(2)}, u32[]{:S(2)}) async-start(bf16[64,2,4,4096]{3,2,1,0:T(4,128)(2,1)} %bitcast.55), calls=%async_computation | async-start | bytes 8388608 | tf_op jit(solution)/shard_map/all_to_all | solution.py:37
  29.7 0.0 reduce-scatter.2.cloned.1.call-start
  29.8 1.2 constant_dynamic-slice_fusion
  31.0 0.6 compare_convert_fusion
  31.7 0.1 broadcast_bitcast_fusion
  31.8 0.0 copy-done.1
  31.8 0.2 convert_reduce_fusion
  32.0 0.4 multiply_reduce_fusion.4
  32.4 0.0 copy-done.3
  32.4 0.3 multiply_convert_fusion.1
  32.7 131.8 %all-to-all-done = bf16[64,2,4,4096]{3,2,1,0:T(4,128)(2,1)} async-done(((bf16[64,2,4,4096]{3,2,1,0:T(4,128)(2,1)}), bf16[64,2,4,4096]{3,2,1,0:T(4,128)(2,1)}, u32[]{:S(2)}, u32[]{:S(2)}) %all-to-all-start) | async-done | bytes 4194336 | tf_op jit(solution)/shard_map/all_to_all | solution.py:37
  164.5 4.5 fusion
  169.0 0.1 copy.21
  169.1 0.1 copy.22
  169.2 0.1 rsqrt.35
  169.3 6.7 %convert_bitcast_fusion = f32[1,2,64,4,4096]{4,3,1,2,0:T(4,128)} fusion(bf16[64,2,4,4096]{3,2,1,0:T(4,128)(2,1)} %all-to-all-done), kind=kLoop, calls=%fused_computation.2 | loop fusion | flops 2097152 | bytes 12582912 | tf_op jit(solution)/shard_map/convert_element_type | solution.py:14
  176.0 7.7 %copy.20 = f32[1,2,64,4,4096]{4,3,2,1,0:T(4,128)} copy(f32[1,2,64,4,4096]{4,3,1,2,0:T(4,128)} %convert_bitcast_fusion) | data formatting | bytes 16777216 | tf_op jit(solution)/shard_map/convert_element_type | solution.py:14
  183.7 10.0 %reshape.160 = f32[512,4096]{1,0:T(8,128)} reshape(f32[1,2,64,4,4096]{4,3,2,1,0:T(4,128)} %copy.20) | data formatting | bytes 16777216 | tf_op jit(solution)/shard_map/convert_element_type | solution.py:14
  193.7 2.1 all-gather.2.cloned.1.call-done
  195.8 0.0 slice-start
  195.8 0.0 slice-start.1
  195.8 8.4 %multiply_reduce_fusion = (f32[512]{0:T(512)S(1)}, f32[512]{0:T(512)S(1)}, f32[512,4096]{1,0:T(8,128)S(1)}) fusion(f32[512,4096]{1,0:T(8,128)} %reshape.160, bf16[512,768]{1,0:T(8,128)(2,1)S(1)} %bitcast.56, bf16[1,4096,768]{2,1,0:T(8,128)(2,1)} %all-gather.2.cloned.1.call-done), kind=kOutput, calls=%fused_computation.6 | convolution fusion | flops 3229613056 | bytes 23859200 | tf_op jit(solution)/shard_map/dot_general | solution.py:47
  204.2 0.6 fusion.13
  204.8 0.0 slice-done
  204.8 0.0 slice-done.1
  204.8 0.0 copy-start.2
  204.8 2.7 fusion.1
  207.5 0.1 copy-done.2
  207.6 3.7 multiply_reduce_fusion.2
  211.3 5.5 %convolution_convert_fusion = bf16[4096,768]{1,0:T(8,128)(2,1)} fusion(bf16[512,4096]{1,0:T(8,128)(2,1)S(1)} %fusion.1, bf16[512,768]{1,0:T(8,128)(2,1)S(1)} %get-tuple-element.12), kind=kOutput, calls=%fused_computation.8 | convolution fusion | flops 3224371200 | bytes 11272192 | tf_op jit(solution)/shard_map/dot_general | solution.py:56
  216.8 0.0 reduce-scatter.2.cloned.1.call-update
  217.5 108.7 %all-reduce = (f32[1]{0:T(128)}, f32[1,768]{1,0:T(1,128)}) all-reduce(f32[1]{0:T(128)} %bitcast.8, f32[1,768]{1,0:T(1,128)S(1)} %reshape.159), channel_id=1, replica_groups=mesh['teacher'=4,'group'=8,'dp'=8] {'teacher','dp'}, use_global_device_ids=true, to_apply=%region_6.0 | all-reduce | flops 769 | bytes 6152 | tf_op jit(solution)/shard_map/psum | solution.py:64
  326.2 0.7 fusion.18
  326.9 1.0 add_convert_fusion
  327.9 169.6 %reduce-scatter.2.cloned.1.call-done = bf16[128,768]{1,0:T(8,128)(2,1)} async-done(((bf16[4096,768]{1,0:T(8,128)(2,1)}), bf16[128,768]{1,0:T(8,128)(2,1)}) %reduce-scatter.2.cloned.1.call-update) | async-done | bytes 196624 | tf_op jit(solution)/shard_map/reduce_scatter | solution.py:55
  497.5 1.7 bitcast_convert_fusion
  (14 shorter events, 0.1 us)
Async XLA Ops:
  7.2 1.7 copy-start
  7.2 188.6 %all-gather.2.cloned.1.call-start = ((), (), s32[]{:S(2)}) async-start(), calls=%async_computation.2 | async-start | bytes 6488064 | tf_op jit(solution)/shard_map/all_gather | solution.py:46
  16.4 15.4 %copy-start.1 = (bf16[1,1,1,2,256,768]{5,4,3,2,1,0:T(8,128)(2,1)S(1)}, bf16[1,1,1,2,256,768]{5,4,3,2,1,0:T(8,128)(2,1)}, u32[]{:S(2)}) copy-start(bf16[1,1,1,2,256,768]{5,4,3,2,1,0:T(8,128)(2,1)} %param.7) | copy-start | bytes 2359300
  16.4 16.0 %copy-start.3 = (f32[1,768]{1,0:T(1,128)S(1)}, f32[1,768]{1,0:T(1,128)}, u32[]{:S(2)}) copy-start(f32[1,768]{1,0:T(1,128)} %param.8) | copy-start | bytes 9220
  16.4 148.1 %all-to-all-start = ((bf16[64,2,4,4096]{3,2,1,0:T(4,128)(2,1)}), bf16[64,2,4,4096]{3,2,1,0:T(4,128)(2,1)}, u32[]{:S(2)}, u32[]{:S(2)}) async-start(bf16[64,2,4,4096]{3,2,1,0:T(4,128)(2,1)} %bitcast.55), calls=%async_computation | async-start | bytes 8388608 | tf_op jit(solution)/shard_map/all_to_all | solution.py:37
  29.7 467.8 %reduce-scatter.2.cloned.1.call-start = ((), (), s32[]{:S(2)}) async-start(), calls=%async_computation.3 | async-start | bytes 6488064 | tf_op jit(solution)/shard_map/reduce_scatter | solution.py:55
  195.8 9.0 %slice-start = ((s8[8388608]{0:T(1024)(128)(4,1)}), s8[4194304]{0:T(1024)(128)(4,1)S(1)}, s32[]{:S(2)}) async-start(s8[8388608]{0:T(1024)(128)(4,1)} %bitcast.53), calls=%async_computation.4 | async-start | bytes 8388608
  195.8 9.0 %slice-start.1 = ((s8[8388608]{0:T(1024)(128)(4,1)}), s8[4194304]{0:T(1024)(128)(4,1)S(1)}, s32[]{:S(2)}) async-start(s8[8388608]{0:T(1024)(128)(4,1)} %bitcast.53), calls=%async_computation.5 | async-start | bytes 8388608
  204.8 2.8 copy-start.2
Sparse Core Ops, SparseCore 0:
  11.5 184.2 all-gather.1
  216.9 280.5 reduce-scatter.1
where the time goes:
time: 507 us; the launch traced here: 506 us
  waiting for transfers between devices  304 us (60%)
  blocking collectives  109 us (21%)
  local copies, waits for them, and re-layouts  27.9 us (6%)
  other arithmetic  19.5 us (4%)
  matrix products  17.5 us (3%)
  between operations  14.8 us (3%)
  starting transfers between devices  13.4 us (3%)
    reduce_scatter x1, waiting for transfers between devices, shards(): lax.psum_scatter(lax.dot_general(dlogits, normed_b, (((0,), (0,)), ((), (...  170 us
    all_to_all x1, waiting for transfers between devices, shards(): lax.all_to_all(direct, ('group', 'dp'), split_axis=0, concat_axis=2, tile...  132 us
    psum x1, blocking collectives, shards(): loss_sum, gain_sum = lax.psum((loss_local, grad_gain), ('teacher', 'dp'))  109 us
    convert_element_type x2, local copies, waits for them, and re-layouts, token_terms(): target32 = target.astype(jnp.float32)  17.7 us
    all_to_all x1, starting transfers between devices, shards(): lax.all_to_all(direct, ('group', 'dp'), split_axis=0, concat_axis=2, tile...  13.3 us
  transfers between devices with their start and end apart: 3, of which 3 were waited for; matrix products, arithmetic and copies ran while one was open for 8% of the time, Pallas kernels for 0%

commit v1 on v0

v1 whole, which is shorter than its diff:
```python
import jax
import jax.numpy as jnp
from jax import lax
from jax.experimental import pallas as pl
from jax.experimental.pallas import tpu as pltpu
from jax.sharding import PartitionSpec as P

MESH = pl.DeviceIdType.MESH
F32 = jnp.float32
BF16 = jnp.bfloat16

FEAT = 4096
WIDTH = 768
PATCHES = 256
SLICE = 1024
MAIN = 256
EXT = 64
BLOCK = MAIN + EXT
ROWS = 4 * BLOCK
TOTAL = 32 * PATCHES
SEMS = 96


def permutation(size, source_of):
    rows = lax.broadcasted_iota(jnp.int32, (size, size), 0)
    cols = lax.broadcasted_iota(jnp.int32, (size, size), 1)
    return jnp.where(source_of(rows) == cols, 1.0, 0.0).astype(BF16)


def image_order(n):
    return (n // 4 % 4) * 32 + (n // 16) * 4 + n % 4


def patch_order(n):
    return (n // 32) * 32 + (n // 4 % 4) * 8 + (n // 16 % 2) * 4 + n % 4


def dot(a, b, dims):
    return lax.dot_general(a, b, (dims, ((), ())), preferred_element_type=F32)


def kernel(
    teach, feats, gain, head, info,
    small_o, sgrad_o, hgrad_o,
    arrived, target, heads, rows_b, extra_out, extra_in,
    xhat, rstd, logits, dlogits, sums, cols,
    stat_out, stat_in, tiny_out, tiny_in,
    g_out, g_own, g_in, gz_out, gz_in,
    d_out, d_own, d_in, e_out, e_in,
    send_sem, recv_sem,
):
    t = lax.axis_index("teacher")
    g = lax.axis_index("group")
    d = lax.axis_index("dp")
    x, zh = d // 2, d % 2
    zl, core = g // 2, g % 2
    z = zh * 4 + zl

    def device(dx=0, dy=0, dz=0, dc=0):
        to_z = (z + dz + 8) % 8
        return {
            "teacher": (t + dy + 4) % 4,
            "group": (to_z % 4) * 2 + (core + dc) % 2,
            "dp": ((x + dx + 4) % 4) * 2 + to_z // 4,
        }

    used = [0]
    copies = []

    def send(src, dst, to):
        index = used[0]
        used[0] += 1
        copy = pltpu.make_async_remote_copy(
            src_ref=src, dst_ref=dst, send_sem=send_sem.at[index], recv_sem=recv_sem.at[index],
            device_id=to, device_id_type=MESH,
        )
        copy.start()
        copies.append(copy)
        return copy

    barrier = pltpu.get_barrier_semaphore()
    partners = [device(dx=k) for k in (1, 2, 3)] + [device(dy=k) for k in (1, 2, 3)]
    partners += [device(dz=k) for k in (1, -1, 4)] + [device(dc=1)]
    for to in partners:
        pl.semaphore_signal(barrier, inc=1, device_id=to, device_id_type=MESH)
    pl.semaphore_wait(barrier, len(partners))

    mine = t * 2 + zh
    head_z = send(head, heads.at[mine], device(dz=4))
    slices = [send(teach.at[(x + k) % 4], arrived.at[x], device(dx=k)) for k in (1, 3, 2)]
    head_y = [send(head, heads.at[mine], device(dy=k)) for k in (1, 3, 2)]
    heads[mine] = head[...]
    arrived[x] = teach[x]

    count = info[128 + g * 8 + d]
    second = jnp.where(count >= 2, 1.0, 0.0).astype(F32)
    order = permutation(MAIN, patch_order)
    base = pl.multiple_of(x * BLOCK, BLOCK)
    for slot in range(2):
        part = pl.ds(slot * MAIN, MAIN)
        values = dot(order, feats[part, :], ((1,), (0,)))
        center = values - jnp.mean(values, axis=-1, keepdims=True)
        rs = lax.rsqrt(jnp.mean(center * center, axis=-1, keepdims=True) + 1e-06)
        unit = center * rs
        xhat[part, :] = unit
        rstd[part, :] = jnp.broadcast_to(rs, (MAIN, 128))
        normed = unit * gain[...]
        if slot == 0:
            rows_b[pl.ds(base, MAIN), :] = normed.astype(BF16)
            here = rows_b.at[pl.ds(base, MAIN), :]
            ring = [send(here, here, device(dx=k)) for k in (1, -1)]
        else:
            extra_out[...] = (normed * second).astype(BF16)
    parts = [
        send(
            extra_out.at[pl.ds(pl.multiple_of((x + k) % 4 * EXT, EXT), EXT), :],
            extra_in.at[k - 1], device(dx=k),
        )
        for k in (1, 3, 2)
    ]

    for copy in slices:
        copy.wait_recv()
    own = dot(permutation(128, image_order), arrived[...].reshape(128, SLICE), ((1,), (0,)))
    block = zl * 4 + core * 2 + zh
    target[:, block] = own.astype(BF16).reshape(8, 16, SLICE)

    def chunk(step, half):
        at = (z + step + 8) % 8
        return target.at[pl.ds(half * 4, 4), (at % 4) * 4 + core * 2 + at // 4]

    shared = []

    def pass_on(step, half, ways):
        piece = chunk(step, half)
        found = [send(piece, piece, device(dz=way)) for way in ways]
        shared.append(send(piece, piece, device(dc=1)))
        return found

    first = [pass_on(0, half, (1, -1)) for half in range(2)]
    from_low = [first[0][0], first[1][0]]
    from_high = [first[0][1], first[1][1]]

    head_z.wait_recv()
    theirs = t * 2 + 1 - zh
    there = heads.at[theirs]
    head_y += [send(there, there, device(dy=k)) for k in (1, 3, 2)]

    for copy in parts:
        copy.wait_recv()
    mine_q = extra_out[pl.ds(pl.multiple_of(x * EXT, EXT), EXT), :].astype(F32)
    mine_q += extra_in[0].astype(F32) + extra_in[1].astype(F32) + extra_in[2].astype(F32)
    rows_b[pl.ds(base + MAIN, EXT), :] = mine_q.astype(BF16)
    tail = rows_b.at[pl.ds(base + MAIN, EXT), :]
    tails = [send(tail, tail, device(dx=k)) for k in (1, 3, 2)]

    def ring_step(step):
        last = step == 3
        for half in range(2):
            from_low[half].wait_recv()
            ways = () if last and half == 1 else (1,)
            found = pass_on(-step, half, ways)
            from_low[half] = found[0] if found else None
            from_high[half].wait_recv()
            ways = () if last and half == 0 else (-1,)
            found = pass_on(step, half, ways)
            from_high[half] = found[0] if found else None

    ring_step(1)

    for copy in ring:
        copy.wait_recv()
    left = rows_b.at[pl.ds(pl.multiple_of((x + 3) % 4 * BLOCK, BLOCK), MAIN // 2), :]
    right = rows_b.at[pl.ds((x + 1) % 4 * BLOCK + MAIN // 2, MAIN // 2), :]
    ring = [send(left, left, device(dx=1)), send(right, right, device(dx=-1))]

    ring_step(2)
    for copy in head_y:
        copy.wait_recv()
    ring_step(3)
    for copy in ring + tails:
        copy.wait_recv()

    def forward(b, carry):
        at = pl.ds(pl.multiple_of(b * BLOCK, BLOCK), BLOCK)
        logits[at, :] = dot(rows_b[at, :], heads[...].reshape(SLICE, WIDTH), ((1,), (1,)))
        return carry

    lax.fori_loop(0, 4, forward, 0)

    from_low[0].wait_recv()
    pass_on(-4, 0, ())
    from_high[1].wait_recv()
    pass_on(4, 1, ())
    for copy in shared:
        copy.wait_recv()

    counts = [info[128 + g * 8 + b * 2 + zh] for b in range(4)]
    extra_image = jnp.int32(0)
    extra_weight = jnp.float32(0)
    main_weight = []
    for b in range(4):
        twice = counts[b] >= 2
        extra_image += jnp.where(twice, info[g * 16 + b * 4 + zh * 2 + 1], 0)
        extra_weight += jnp.where(twice, 1.0, 0.0).astype(F32)
        main_weight.append(jnp.where(counts[b] >= 1, 1.0, 0.0).astype(F32))

    def targets(b):
        image = info[g * 16 + b * 4 + zh * 2]
        main = target[image].reshape(MAIN, SLICE)
        ext = target[extra_image, pl.ds(b * 4, 4)].reshape(EXT, SLICE)
        return jnp.concatenate([main, ext], axis=0).astype(F32)

    lane = lax.broadcasted_iota(jnp.int32, (BLOCK, 128), 1)

    def statistics(b, carry):
        at = pl.ds(pl.multiple_of(b * BLOCK, BLOCK), BLOCK)
        lg = logits[at, :]
        tg = targets(b)
        inner = jnp.sum(lg * tg, axis=-1, keepdims=True)
        lsq = jnp.sum(lg * lg, axis=-1, keepdims=True)
        tsq = jnp.sum(tg * tg, axis=-1, keepdims=True)
        sums[at, :] = jnp.where(lane == 0, inner, jnp.where(lane == 1, lsq, tsq))
        return carry

    lax.fori_loop(0, 4, statistics, 0)
    for k in range(ROWS // 128):
        stat_out[:, k * 128:(k + 1) * 128] = jnp.transpose(sums[k * 128:(k + 1) * 128, :])[:8]
    stats = [send(stat_out, stat_in.at[k - 1], device(dx=k)) for k in (1, 3, 2)]
    for copy in stats:
        copy.wait_recv()
    total = (stat_out[...] + stat_in[0] + stat_in[1] + stat_in[2]) * (1.0 / FEAT)
    inner, lsq, tsq = total[0:1], total[1:2], total[2:3]
    rl, rt = lax.rsqrt(lsq + 1e-06), lax.rsqrt(tsq + 1e-06)
    row = lax.broadcasted_iota(jnp.int32, (1, ROWS), 1)
    weight = jnp.zeros((1, ROWS), F32)
    for b in range(4):
        low = b * BLOCK
        weight = jnp.where((row >= low) & (row < low + MAIN), main_weight[b], weight)
        weight = jnp.where((row >= low + MAIN) & (row < low + BLOCK), extra_weight, weight)
    here = (row >= x * BLOCK) & (row < x * BLOCK + BLOCK)
    loss = jnp.sum(jnp.where(here, weight * (1.0 - inner * rl * rt), 0.0)) * (1.0 / TOTAL)
    on_target = weight * rl * rt * (-1.0 / 16.0)
    on_logits = weight * inner * rt * rl * rl * rl * (1.0 / 16.0)
    pair = jnp.concatenate([on_target, on_logits, jnp.zeros((126, ROWS), F32)], axis=0)
    for k in range(ROWS // 128):
        cols[k * 128:(k + 1) * 128, :] = jnp.transpose(pair[:, k * 128:(k + 1) * 128])

    def backward(b, carry):
        at = pl.ds(pl.multiple_of(b * BLOCK, BLOCK), BLOCK)
        factors = cols[at, :]
        dl = factors[:, 0:1] * targets(b) + factors[:, 1:2] * logits[at, :]
        dlogits[at, :] = dl.astype(BF16)
        return carry

    lax.fori_loop(0, 4, backward, 0)

    gain_part = jnp.zeros((1, WIDTH), F32)
    away, near = [], []
    far = pl.ds(pl.multiple_of((1 - zh) * 128, 128), 128)
    close = pl.ds(pl.multiple_of(zh * 128, 128), 128)
    for k in (2, 1, 3, 0):
        to = (t + k) % 4
        columns = pl.ds(pl.multiple_of(to * 256, 256), 256)
        part = dot(dlogits[:, columns], rows_b[...], ((0,), (0,)))
        weights = heads[pl.ds(to * 2, 2)].reshape(256, WIDTH).astype(F32)
        gain_part += jnp.sum(part * weights, axis=0, keepdims=True)
        if k:
            g_out[k - 1] = part.astype(BF16)
            away.append(send(g_out.at[k - 1, far], g_in.at[0, k - 1], device(dy=k)))
        else:
            g_own[...] = part
    for k in (2, 1, 3):
        near.append(send(g_out.at[k - 1, close], g_in.at[1, k - 1], device(dy=k)))

    which = lax.broadcasted_iota(jnp.int32, (8, WIDTH), 0)
    tiny = jnp.where(which == 0, gain_part / gain[...], jnp.where(which == 1, loss, 0.0))
    tiny_out[0] = tiny
    tiny_x = [send(tiny_out.at[0], tiny_in.at[k - 1], device(dx=k)) for k in (1, 3, 2)]

    ext_parts, main_parts = [], []
    for k in (2, 1, 3, 0):
        at = pl.ds(pl.multiple_of((x + k) % 4 * BLOCK, BLOCK), BLOCK)
        part = dot(dlogits[at, :], heads[...].reshape(SLICE, WIDTH), ((1,), (0,)))
        if k:
            d_out[k - 1] = part.astype(BF16)
            rest = pl.ds(MAIN, EXT)
            ext_parts.append(send(d_out.at[k - 1, rest], d_in.at[k - 1, rest], device(dx=k)))
        else:
            d_own[...] = part
    for k in (2, 1, 3):
        rest = pl.ds(0, MAIN)
        main_parts.append(send(d_out.at[k - 1, rest], d_in.at[k - 1, rest], device(dx=k)))

    for copy in tiny_x:
        copy.wait_recv()
    tiny += tiny_in[0] + tiny_in[1] + tiny_in[2]
    tiny_out[1] = tiny
    tiny_y = [send(tiny_out.at[1], tiny_in.at[2 + k], device(dy=k)) for k in (1, 3, 2)]

    for copy in ext_parts:
        copy.wait_recv()
    rest = pl.ds(MAIN, EXT)
    ext_sum = d_own[rest, :]
    for k in range(3):
        ext_sum += d_in[k, rest].astype(F32)
    e_out[...] = ext_sum.astype(BF16)
    ext_all = [send(e_out, e_in.at[k - 1], device(dx=k)) for k in (1, 3, 2)]

    for copy in away:
        copy.wait_recv()
    part = g_own[far, :]
    for k in range(3):
        part += g_in[0, k].astype(F32)
    gz_out[...] = part.astype(BF16)
    across = send(gz_out, gz_in, device(dz=4))

    for copy in tiny_y:
        copy.wait_recv()
    tiny += tiny_in[3] + tiny_in[4] + tiny_in[5]
    tiny_out[2] = tiny
    tiny_z = send(tiny_out.at[2], tiny_in.at[6], device(dz=4))

    def finish(dnormed, part):
        dx = dnormed * gain[...]
        unit = xhat[part, :]
        drop = jnp.mean(dx, axis=-1, keepdims=True)
        along = jnp.mean(dx * unit, axis=-1, keepdims=True)
        out = (rstd[part, :][:, 0:1] * (dx - drop - unit * along)).astype(BF16)
        sgrad_o[part, :] = dot(order, out, ((0,), (0,))).astype(BF16)

    for copy in ext_all:
        copy.wait_recv()
    quarters = []
    for q in range(4):
        got = jnp.where(x == q, ext_sum, 0.0)
        for k in (1, 2, 3):
            got = jnp.where((x + 4 - k) % 4 == q, e_in[k - 1].astype(F32), got)
        quarters.append(got * second)
    finish(jnp.concatenate(quarters, axis=0), pl.ds(MAIN, MAIN))

    for copy in main_parts:
        copy.wait_recv()
    rest = pl.ds(0, MAIN)
    dn = d_own[rest, :]
    for k in range(3):
        dn += d_in[k, rest].astype(F32)
    finish(dn, rest)

    for copy in near:
        copy.wait_recv()
    part = g_own[close, :]
    for k in range(3):
        part += g_in[1, k].astype(F32)
    across.wait_recv()
    hgrad_o[...] = part + gz_in[...].astype(F32)
    tiny_z.wait_recv()
    small_o[...] = tiny + tiny_in[6]
    for copy in copies:
        copy.wait_send()


def shards(teacher_feats, student_feats, norm_gain, head_weight, slot_image, slot_count):
    by_slice = teacher_feats.reshape(32, 4, 4, 256).transpose(2, 0, 1, 3).reshape(4, 32, SLICE)
    info = jnp.concatenate([slot_image.reshape(-1), slot_count.reshape(-1)])
    vmem = pl.BlockSpec(memory_space=pltpu.VMEM)
    smem = pl.BlockSpec(memory_space=pltpu.SMEM)
    small, sgrad, hgrad = pl.pallas_call(
        kernel,
        out_shape=(
            jax.ShapeDtypeStruct((8, WIDTH), F32),
            jax.ShapeDtypeStruct((2 * MAIN, WIDTH), BF16),
            jax.ShapeDtypeStruct((128, WIDTH), F32),
        ),
        in_specs=[vmem, vmem, vmem, vmem, smem],
        out_specs=(vmem, vmem, vmem),
        scratch_shapes=[
            pltpu.VMEM((4, 32, SLICE), BF16),
            pltpu.VMEM((8, 16, 16, SLICE), BF16),
            pltpu.VMEM((8, 128, WIDTH), BF16),
            pltpu.VMEM((ROWS, WIDTH), BF16),
            pltpu.VMEM((MAIN, WIDTH), BF16),
            pltpu.VMEM((3, EXT, WIDTH), BF16),
            pltpu.VMEM((2 * MAIN, WIDTH), F32),
            pltpu.VMEM((2 * MAIN, 128), F32),
            pltpu.VMEM((ROWS, SLICE), F32),
            pltpu.VMEM((ROWS, SLICE), BF16),
            pltpu.VMEM((ROWS, 128), F32),
            pltpu.VMEM((ROWS, 128), F32),
            pltpu.VMEM((8, ROWS), F32),
            pltpu.VMEM((3, 8, ROWS), F32),
            pltpu.VMEM((3, 8, WIDTH), F32),
            pltpu.VMEM((7, 8, WIDTH), F32),
            pltpu.VMEM((3, 256, WIDTH), BF16),
            pltpu.VMEM((256, WIDTH), F32),
            pltpu.VMEM((2, 3, 128, WIDTH), BF16),
            pltpu.VMEM((128, WIDTH), BF16),
            pltpu.VMEM((128, WIDTH), BF16),
            pltpu.VMEM((3, BLOCK, WIDTH), BF16),
            pltpu.VMEM((BLOCK, WIDTH), F32),
            pltpu.VMEM((3, BLOCK, WIDTH), BF16),
            pltpu.VMEM((EXT, WIDTH), BF16),
            pltpu.VMEM((3, EXT, WIDTH), BF16),
            pltpu.SemaphoreType.DMA((SEMS,)),
            pltpu.SemaphoreType.DMA((SEMS,)),
        ],
        compiler_params=pltpu.CompilerParams(
            collective_id=0, has_side_effects=True, vmem_limit_bytes=56 << 20
        ),
        name="head_step",
    )(by_slice, student_feats.reshape(2 * MAIN, WIDTH), norm_gain, head_weight.reshape(128, WIDTH), info)
    return (
        small[1, 0:1],
        sgrad.reshape(student_feats.shape),
        hgrad.reshape(1, 128, WIDTH),
        small[0:1],
    )


def solution(mesh):
    return jax.shard_map(
        shards,
        mesh=mesh,
        in_specs=(
            P("teacher", ("group", "dp"), None),
            P("group", "teacher", "dp", None, None, None),
            P("group", None),
            P("group", ("teacher", "dp"), None),
            P(None, "teacher", None, None),
            P(None, "teacher", None),
        ),
        out_specs=(
            P("group"),
            P("group", "teacher", "dp", None, None, None),
            P("group", ("teacher", "dp"), None),
            P("group", None),
        ),
        check_vma=False,
    )
```

time: 507 us -> 101 us (0.20)
  waiting for transfers between devices: 304 us -> 0 us
  blocking collectives: 109 us -> 0 us
  Pallas kernels: 0 us -> 90.7 us
  local copies, waits for them, and re-layouts: 27.9 us -> 8.4 us
  other arithmetic: 19.5 us -> 1.23 us
  matrix products: 17.5 us -> 0 us
  between operations: 14.8 us -> 0.68 us
  starting transfers between devices: 13.4 us -> 0 us
    reduce_scatter x1 -> x0, waiting for transfers between devices: 170 us -> none  [shards(): lax.psum_scatter(lax.dot_general(dlogits, normed_b, (((0,), (0,)), ((), (...]
    all_to_all x1 -> x0, waiting for transfers between devices: 132 us -> none  [shards(): lax.all_to_all(direct, ('group', 'dp'), split_axis=0, concat_axis=2, tile...]
    psum x1 -> x0, blocking collectives: 109 us -> none  [shards(): loss_sum, gain_sum = lax.psum((loss_local, grad_gain), ('teacher', 'dp'))]
    pallas_call x0 -> x1, Pallas kernels: none -> 90.7 us  [shards(): pl.pallas_call(kernel, out_shape=(jax.ShapeDtypeStruct((8, WIDTH), F32),...]
    convert_element_type x2 -> x0, local copies, waits for them, and re-layouts: 17.7 us -> none  [token_terms(): target32 = target.astype(jnp.float32)]
    dot_general x3 -> x0, matrix products: 17.5 us -> none  [the longest x1 8.39 us: shards(): lax.dot_general(normed_b, whole_head, (((1,), (1,)), ((), ())), preferred...]
    all_to_all x1 -> x0, starting transfers between devices: 13.3 us -> none  [shards(): lax.all_to_all(direct, ('group', 'dp'), split_axis=0, concat_axis=2, tile...]
    convert_element_type x5 -> x0, other arithmetic: 11.4 us -> none  [the longest x1 6.69 us: token_terms(): target32 = target.astype(jnp.float32)]
  transfers between devices with their start and end apart: 3 -> 0, of which waited for: 3 -> 0; matrix products, arithmetic and copies ran while one was open for 8% -> 0% of each run, Pallas kernels for 0% -> 0%
where the time goes in v1:
time: 101 us
  Pallas kernels  90.7 us (90%)
  local copies, waits for them, and re-layouts  8.4 us (8%)
  other arithmetic  1.23 us (1%)
    pallas_call x1, Pallas kernels, shards(): pl.pallas_call(kernel, out_shape=(jax.ShapeDtypeStruct((8, WIDTH), F32),...  90.7 us
    unnamed x10, local copies, waits for them, and re-layouts  3.54 us
    reshape x3, local copies, waits for them, and re-layouts, shards(): teacher_feats.reshape(32, 4, 4, 256).transpose(2, 0, 1, 3)  2.15 us

profile of v1, /device:TPU:1, one launch (start us, length us, event | category | flops | bytes accessed | tf_op | source)
XLA Modules:
  0.0 101.0 jit_solution(15009291525416372494)
XLA Ops:
  0.6 1.2 %reshape.32 = bf16[32,4,4,256]{3,2,1,0:T(4,128)(2,1)S(1)} reshape(bf16[8,4,4096]{2,1,0:T(4,128)(2,1)} %param.6) | data formatting | bytes 524288 | tf_op jit(solution)/shard_map/reshape | solution.py:364
  1.8 0.1 copy.15
  1.9 0.0 copy-start.1
  1.9 0.9 reshape.33.teach
  2.8 0.0 copy-done.1
  2.8 0.1 copy.13
  2.9 0.0 copy-start.2
  2.9 0.1 reshape.36
  3.1 0.5 broadcast.3
  3.6 0.0 copy-done.2
  3.6 0.7 reduce.3
  4.3 0.1 reshape.37
  4.4 0.6 pad_add_fusion.info
  4.9 90.7 %head_step.1 = (f32[8,768]{1,0:T(8,128)}, bf16[512,768]{1,0:T(8,128)(2,1)}, f32[128,768]{1,0:T(8,128)}) custom-call(bf16[4,32,1024]{2,1,0:T(8,128)(2,1)} %reshape.33.teach, bf16[512,768]{1,0:T(8,128)(2,1)} %bitcast.13, f32[1,768]{1,0:T(1,128)} %gain.1, bf16[128,768]{1,0:T(8,128)(2,1)} %bitcast.16, s32[192]{0:T(256)} %pad_add_fusion.info), custom_call_target="tpu_custom_call" | custom-call | tf_op jit(solution)/shard_map/head_step/pallas_call | solution.py:368
  95.7 1.3 %slice.7 = f32[1,768]{1,0:T(1,128)} slice(f32[8,768]{1,0:T(8,128)} %get-tuple-element.7), slice={[0:1], [0:768]} | slice | bytes 6144 | tf_op jit(solution)/shard_map/slice | solution.py:416
  97.0 1.2 %slice.6 = f32[1,1]{1,0:T(1,128)} slice(f32[8,768]{1,0:T(8,128)} %get-tuple-element.7), slice={[1:2], [0:1]} | slice | bytes 8 | tf_op jit(solution)/shard_map/slice | solution.py:413
  98.2 0.0 copy-start
  98.2 2.1 %copy.18 = bf16[1,1,1,2,256,768]{5,4,3,2,1,0:T(8,128)(2,1)} copy(bf16[1,1,1,2,256,768]{5,4,3,2,1,0:T(8,128)(2,1)} %bitcast.14) | data formatting | bytes 1572864
  100.3 0.0 copy-done
  100.3 0.7 copy.19
Async XLA Ops:
  1.9 0.9 copy-start.1
  2.9 0.7 copy-start.2
  98.2 2.1 %copy-start = (f32[128,768]{1,0:T(8,128)S(1)}, f32[128,768]{1,0:T(8,128)}, u32[]{:S(2)}) copy-start(f32[128,768]{1,0:T(8,128)} %get-tuple-element.9) | copy-start | bytes 1179652

commit v2 on v1

v2 whole, which is shorter than its diff:
```python
import jax
import jax.numpy as jnp
from jax import lax
from jax.experimental import pallas as pl
from jax.experimental.pallas import tpu as pltpu
from jax.sharding import PartitionSpec as P

MESH = pl.DeviceIdType.MESH
F32 = jnp.float32
BF16 = jnp.bfloat16

FEAT = 4096
WIDTH = 768
PATCHES = 256
SLICE = 1024
MAIN = 256
PART = 32
GROUP = 640
TOTAL = 32 * PATCHES
SEMS = 104


def permutation(size, source_of):
    rows = lax.broadcasted_iota(jnp.int32, (size, size), 0)
    cols = lax.broadcasted_iota(jnp.int32, (size, size), 1)
    return jnp.where(source_of(rows) == cols, 1.0, 0.0).astype(BF16)


def image_order(n):
    return (n // 4 % 4) * 32 + (n // 16) * 4 + n % 4


def dot(a, b, dims):
    return lax.dot_general(a, b, (dims, ((), ())), preferred_element_type=F32)


def kernel(
    teach, feats, gain, head, images, used_slots,
    loss_o, gain_o, sgrad_o, hgrad_o,
    arrived, near_target, far_target, heads, rows_b, extra_out, extra_in,
    xhat, rstd, logits, dlogits, sums, cols,
    stat_out, stat_in, tiny_out, tiny_in,
    g_out, g_own, g_in, gz_out, gz_in,
    d_all, d_out, d_in, e_in, e_all,
    feats_v, send_sem, recv_sem, local_sem,
):
    t = lax.axis_index("teacher")
    g = lax.axis_index("group")
    d = lax.axis_index("dp")
    x, zh = d // 2, d % 2
    zl, core = g // 2, g % 2
    z = zh * 4 + zl

    def device(dx=0, dy=0, dz=0, dc=0):
        to_z = (z + dz + 8) % 8
        return {
            "teacher": (t + dy + 4) % 4,
            "group": (to_z % 4) * 2 + (core + dc) % 2,
            "dp": ((x + dx + 4) % 4) * 2 + to_z // 4,
        }

    used = [0]
    copies = []

    def send(src, dst, to):
        index = used[0]
        used[0] += 1
        copy = pltpu.make_async_remote_copy(
            src_ref=src, dst_ref=dst, send_sem=send_sem.at[index], recv_sem=recv_sem.at[index],
            device_id=to, device_id_type=MESH,
        )
        copy.start()
        copies.append(copy)
        return copy

    def arrive(found):
        for copy in found:
            copy.wait_recv()

    barrier = pltpu.get_barrier_semaphore()
    partners = [device(dx=k) for k in (1, 2, 3)] + [device(dy=k) for k in (1, 2, 3)]
    partners += [device(dz=k) for k in (1, -1, 4)] + [device(dc=1)]
    for to in partners:
        pl.semaphore_signal(barrier, inc=1, device_id=to, device_id_type=MESH)

    def patch_order(n):
        h, q, c, xs, p = n // 128, n // 32 % 4, n // 16 % 2, n // 4 % 4, n % 4
        away = jnp.where(q == 1, 7, jnp.where(q == 2, 1, jnp.where(q == 3, 6, 0)))
        at = (z + away + 4 * h) % 8
        return (at % 4) * 64 + c * 32 + xs * 8 + (at // 4) * 4 + p

    mine = t * 2 + zh
    feats_in = pltpu.make_async_copy(feats, feats_v, local_sem.at[0])
    feats_in.start()

    def columns_of(to, b):
        return pl.ds(pl.multiple_of(b * SLICE + to * 256, 256), 256)

    owned = [pltpu.make_async_copy(head, heads.at[mine], local_sem.at[1])]
    for b in range(4):
        owned.append(pltpu.make_async_copy(
            teach.at[:, columns_of(x, b)], arrived.at[x, :, pl.ds(b * 256, 256)], local_sem.at[2 + b]
        ))
    for copy in owned:
        copy.start()
    feats_in.wait()
    second = jnp.where(used_slots[g, 0, d] >= 2, 1.0, 0.0).astype(F32)
    order = permutation(MAIN, patch_order)
    for slot in range(2):
        part = pl.ds(slot * MAIN, MAIN)
        values = dot(order, feats_v[part, :], ((1,), (0,)))
        center = values - jnp.mean(values, axis=-1, keepdims=True)
        rs = lax.rsqrt(jnp.mean(center * center, axis=-1, keepdims=True) + 1e-06)
        unit = center * rs
        xhat[part, :] = unit
        rstd[part, :] = jnp.broadcast_to(rs, (MAIN, 128))
        normed = unit * gain[...]
        if slot == 0:
            rows_b[:, :, x] = normed.astype(BF16).reshape(2, 4, PART, WIDTH)
        else:
            extra_out[...] = (normed * second).astype(BF16).reshape(2, 4, PART, WIDTH)
    pl.semaphore_wait(barrier, len(partners))

    slices = []
    for k in (1, 3, 2):
        for b in range(4):
            columns = columns_of((x + k) % 4, b)
            slices.append(send(teach.at[:, columns], arrived.at[x, :, pl.ds(b * 256, 256)], device(dx=k)))
    head_z = send(head, heads.at[mine], device(dz=4))
    parts = [send(extra_out.at[:, (x + k) % 4], extra_in.at[k - 1], device(dx=k)) for k in (1, 3, 2)]
    here = rows_b.at[:, :, x]
    ring = [send(here, here, device(dx=k)) for k in (1, -1)]
    head_y = [send(head, heads.at[mine], device(dy=k)) for k in (1, 3, 2)]

    arrive(slices)
    for copy in owned:
        copy.wait()
    own = dot(permutation(128, image_order), arrived[...].reshape(128, SLICE), ((1,), (0,)))
    target = (near_target, far_target)
    near_target[0, :, core] = own.astype(BF16).reshape(8, 16, SLICE)
    places = {0: (0, 0), -1: (0, 1), 1: (0, 2), -2: (0, 3), 4: (1, 0), -4: (1, 0), 3: (1, 1), -3: (1, 2), 2: (1, 3)}

    def chunk(step, half):
        h, q = places[step]
        return target[h].at[q, pl.ds(half * 4, 4), core]

    shared = [[], []]

    def pass_on(step, half, ways):
        piece = chunk(step, half)
        found = [send(piece, chunk(step - way, half), device(dz=way)) for way in ways]
        shared[places[step][0]].append(send(piece, piece, device(dc=1)))
        return found

    first = [pass_on(0, half, (1, -1)) for half in range(2)]
    from_low = [first[0][0], first[1][0]]
    from_high = [first[0][1], first[1][1]]

    def ring_step(step):
        last = step == 3
        for half in range(2):
            from_low[half].wait_recv()
            ways = () if last and half == 1 else (1,)
            found = pass_on(-step, half, ways)
            from_low[half] = found[0] if found else None
            from_high[half].wait_recv()
            ways = () if last and half == 0 else (-1,)
            found = pass_on(step, half, ways)
            from_high[half] = found[0] if found else None

    arrive(parts)
    quarter = extra_out[:, x].astype(F32)
    quarter += extra_in[0].astype(F32) + extra_in[1].astype(F32) + extra_in[2].astype(F32)
    rows_b[:, x, 4] = quarter.astype(BF16)
    tail = rows_b.at[:, x, 4]
    tails = [send(tail, tail, device(dx=k)) for k in (1, 3, 2)]

    head_z.wait_recv()
    theirs = heads.at[t * 2 + 1 - zh]
    head_y += [send(theirs, theirs, device(dy=k)) for k in (1, 3, 2)]

    ring_step(1)

    arrive(ring)
    left, right = rows_b.at[0, :, (x + 3) % 4], rows_b.at[1, :, (x + 1) % 4]
    ring = [send(left, left, device(dx=1)), send(right, right, device(dx=-1))]
    ring_step(2)
    ring_step(3)
    arrive(head_y)
    arrive(ring)
    arrive(tails)

    extra_image = jnp.int32(0)
    extra_weight = jnp.float32(0)
    image, weights = [], []
    for b in range(4):
        count = used_slots[g, 0, b * 2 + zh]
        twice = count >= 2
        extra_image += jnp.where(twice, images[g, 0, 1, b * 2 + zh], 0)
        extra_weight += jnp.where(twice, 1.0, 0.0).astype(F32)
        image.append(images[g, 0, 0, b * 2 + zh])
        weights.append(jnp.where(count >= 1, 1.0, 0.0).astype(F32))
    image.append(extra_image)
    weights.append(extra_weight)
    row = lax.broadcasted_iota(jnp.int32, (1, GROUP), 1)
    slot_of = (row // PART) % 5
    weight = jnp.zeros((1, GROUP), F32)
    for i in range(5):
        weight = jnp.where(slot_of == i, weights[i], weight)
    here = (slot_of == x) | ((slot_of == 4) & (row // 160 == x))
    loss = jnp.float32(0)

    def targets(h, q):
        found = [target[h][q, image[i]].reshape(PART, SLICE) for i in range(5)]
        return jnp.concatenate(found, axis=0).astype(F32)

    def forward(h):
        def step(b, carry):
            rows = rows_b[h, pl.ds(b * 2, 2)].reshape(320, WIDTH)
            out = dot(rows, heads[...].reshape(SLICE, WIDTH), ((1,), (1,)))
            logits[h, pl.ds(b * 2, 2)] = out.reshape(2, 160, SLICE)
            return carry

        lax.fori_loop(0, 2, step, 0)

    lane = lax.broadcasted_iota(jnp.int32, (160, 128), 1)

    def statistics(h):
        def step(q, carry):
            lg = logits[h, q]
            tg = targets(h, q)
            inner = jnp.sum(lg * tg, axis=-1, keepdims=True)
            lsq = jnp.sum(lg * lg, axis=-1, keepdims=True)
            tsq = jnp.sum(tg * tg, axis=-1, keepdims=True)
            at = pl.ds(pl.multiple_of(q * 160, 32), 160)
            sums[h, at, :] = jnp.where(lane == 0, inner, jnp.where(lane == 1, lsq, tsq))
            return carry

        lax.fori_loop(0, 4, step, 0)
        for k in range(GROUP // 128):
            at = pl.ds(k * 128, 128)
            stat_out[h, :, at] = jnp.transpose(sums[h, at, :])[:8]
        return [send(stat_out.at[h], stat_in.at[k - 1, h], device(dx=k)) for k in (1, 3, 2)]

    def factors(h):
        total = (stat_out[h] + stat_in[0, h] + stat_in[1, h] + stat_in[2, h]) * (1.0 / FEAT)
        inner, lsq, tsq = total[0:1], total[1:2], total[2:3]
        rl, rt = lax.rsqrt(lsq + 1e-06), lax.rsqrt(tsq + 1e-06)
        on_target = weight * rl * rt * (-1.0 / 16.0)
        on_logits = weight * inner * rt * rl * rl * rl * (1.0 / 16.0)
        pair = jnp.concatenate([on_target, on_logits, jnp.zeros((126, GROUP), F32)], axis=0)
        for k in range(GROUP // 128):
            cols[h, k * 128:(k + 1) * 128, :] = jnp.transpose(pair[:, k * 128:(k + 1) * 128])

        def step(q, carry):
            found = cols[h, pl.ds(pl.multiple_of(q * 160, 32), 160), :]
            dl = found[:, 0:1] * targets(h, q) + found[:, 1:2] * logits[h, q]
            dlogits[h, q] = dl.astype(BF16)
            return carry

        lax.fori_loop(0, 4, step, 0)
        return jnp.sum(jnp.where(here, weight * (1.0 - inner * rl * rt), 0.0)) * (1.0 / TOTAL)

    def row_gradient(h):
        def step(b, carry):
            part = dot(dlogits[h, pl.ds(b * 2, 2)].reshape(320, SLICE), heads[...].reshape(SLICE, WIDTH), ((1,), (0,)))
            part = part.reshape(2, 5, PART, WIDTH)
            d_all[h, pl.ds(b * 2, 2)] = part
            d_out[h, pl.ds(b * 2, 2)] = part.astype(BF16)
            return carry

        lax.fori_loop(0, 2, step, 0)
        ext = [send(d_out.at[h, (x + k) % 4, 4], e_in.at[k - 1, h], device(dx=k)) for k in (1, 3, 2)]
        main = [send(d_out.at[h, :, (x + k) % 4], d_in.at[k - 1, h], device(dx=k)) for k in (1, 3, 2)]
        return ext, main

    def extra_sum(h):
        total = d_all[h, x, 4]
        for k in range(3):
            total += e_in[k, h].astype(F32)
        e_all[h, x] = total.astype(BF16)
        piece = e_all.at[h, x]
        return [send(piece, piece, device(dx=k)) for k in (1, 3, 2)]

    forward(0)
    arrive(shared[0])
    stats_a = statistics(0)
    forward(1)
    from_low[0].wait_recv()
    pass_on(-4, 0, ())
    from_high[1].wait_recv()
    pass_on(4, 1, ())
    arrive(shared[1])
    stats_b = statistics(1)
    arrive(stats_a)
    loss += factors(0)
    ext_a, main_a = row_gradient(0)
    arrive(stats_b)
    loss += factors(1)

    gain_part = jnp.zeros((1, WIDTH), F32)
    away, near = [], []
    far = pl.ds(pl.multiple_of((1 - zh) * 128, 128), 128)
    close = pl.ds(pl.multiple_of(zh * 128, 128), 128)
    for k in (2, 1, 3, 0):
        to = (t + k) % 4
        columns = pl.ds(pl.multiple_of(to * 256, 256), 256)
        part = dot(
            dlogits[:, :, :, columns].reshape(2 * GROUP, 256), rows_b[...].reshape(2 * GROUP, WIDTH), ((0,), (0,))
        )
        head_part = heads[pl.ds(to * 2, 2)].reshape(256, WIDTH).astype(F32)
        gain_part += jnp.sum(part * head_part, axis=0, keepdims=True)
        if k:
            g_out[k - 1] = part.astype(BF16)
            away.append(send(g_out.at[k - 1, far], g_in.at[0, k - 1], device(dy=k)))
        else:
            g_own[...] = part
    for k in (2, 1, 3):
        near.append(send(g_out.at[k - 1, close], g_in.at[1, k - 1], device(dy=k)))

    which = lax.broadcasted_iota(jnp.int32, (8, WIDTH), 0)
    tiny = jnp.where(which == 0, gain_part / gain[...], jnp.where(which == 1, loss, 0.0))
    tiny_out[0] = tiny
    tiny_x = [send(tiny_out.at[0], tiny_in.at[k - 1], device(dx=k)) for k in (1, 3, 2)]

    ext_b, main_b = row_gradient(1)

    arrive(tiny_x)
    tiny += tiny_in[0] + tiny_in[1] + tiny_in[2]
    tiny_out[1] = tiny
    tiny_z = send(tiny_out.at[1], tiny_in.at[6], device(dz=4))

    arrive(ext_a)
    ext_all = extra_sum(0)
    arrive(ext_b)
    ext_all += extra_sum(1)

    tiny_z.wait_recv()
    tiny += tiny_in[6]
    tiny_out[2] = tiny
    tiny_y = [send(tiny_out.at[2], tiny_in.at[2 + k], device(dy=k)) for k in (1, 3, 2)]

    arrive(away)
    part = g_own[far, :]
    for k in range(3):
        part += g_in[0, k].astype(F32)
    gz_out[...] = part.astype(BF16)
    across = send(gz_out, gz_in, device(dz=4))

    def finish(dnormed, part):
        dx = dnormed.reshape(MAIN, WIDTH) * gain[...]
        unit = xhat[part, :]
        drop = jnp.mean(dx, axis=-1, keepdims=True)
        along = jnp.mean(dx * unit, axis=-1, keepdims=True)
        out = (rstd[part, :][:, 0:1] * (dx - drop - unit * along)).astype(BF16)
        sgrad_o[part, :] = dot(order, out, ((0,), (0,))).astype(BF16)

    arrive(ext_all)
    finish(e_all[...].astype(F32) * second, pl.ds(MAIN, MAIN))

    arrive(main_a)
    arrive(main_b)
    dn = d_all[:, :, x]
    for k in range(3):
        dn += d_in[k].astype(F32)
    finish(dn, pl.ds(0, MAIN))

    arrive(near)
    part = g_own[close, :]
    for k in range(3):
        part += g_in[1, k].astype(F32)
    across.wait_recv()
    hgrad_o[...] = part + gz_in[...].astype(F32)
    arrive(tiny_y)
    tiny += tiny_in[3] + tiny_in[4] + tiny_in[5]
    gain_o[...] = tiny[0:1]
    loss_o[0] = tiny[1, 0]
    for copy in copies:
        copy.wait_send()


def shards(teacher_feats, student_feats, norm_gain, head_weight, slot_image, slot_count):
    vmem = pl.BlockSpec(memory_space=pltpu.VMEM)
    smem = pl.BlockSpec(memory_space=pltpu.SMEM)
    anywhere = pl.BlockSpec(memory_space=pl.ANY)
    loss, gain_grad, sgrad, hgrad = pl.pallas_call(
        kernel,
        out_shape=(
            jax.ShapeDtypeStruct((1,), F32),
            jax.ShapeDtypeStruct((1, WIDTH), F32),
            pltpu.VMEM((2 * MAIN, WIDTH), BF16),
            pltpu.VMEM((128, WIDTH), F32),
        ),
        in_specs=[anywhere, anywhere, vmem, anywhere, smem, smem],
        out_specs=(smem, vmem, vmem, vmem),
        scratch_shapes=[
            pltpu.VMEM((4, 32, SLICE), BF16),
            pltpu.VMEM((4, 8, 2, 16, SLICE), BF16),
            pltpu.VMEM((4, 8, 2, 16, SLICE), BF16),
            pltpu.VMEM((8, 128, WIDTH), BF16),
            pltpu.VMEM((2, 4, 5, PART, WIDTH), BF16),
            pltpu.VMEM((2, 4, PART, WIDTH), BF16),
            pltpu.VMEM((3, 2, PART, WIDTH), BF16),
            pltpu.VMEM((2 * MAIN, WIDTH), F32),
            pltpu.VMEM((2 * MAIN, 128), F32),
            pltpu.VMEM((2, 4, 160, SLICE), F32),
            pltpu.VMEM((2, 4, 160, SLICE), BF16),
            pltpu.VMEM((2, GROUP, 128), F32),
            pltpu.VMEM((2, GROUP, 128), F32),
            pltpu.VMEM((2, 8, GROUP), F32),
            pltpu.VMEM((3, 2, 8, GROUP), F32),
            pltpu.VMEM((3, 8, WIDTH), F32),
            pltpu.VMEM((7, 8, WIDTH), F32),
            pltpu.VMEM((3, 256, WIDTH), BF16),
            pltpu.VMEM((256, WIDTH), F32),
            pltpu.VMEM((2, 3, 128, WIDTH), BF16),
            pltpu.VMEM((128, WIDTH), BF16),
            pltpu.VMEM((128, WIDTH), BF16),
            pltpu.VMEM((2, 4, 5, PART, WIDTH), F32),
            pltpu.VMEM((2, 4, 5, PART, WIDTH), BF16),
            pltpu.VMEM((3, 2, 4, PART, WIDTH), BF16),
            pltpu.VMEM((3, 2, PART, WIDTH), BF16),
            pltpu.VMEM((2, 4, PART, WIDTH), BF16),
            pltpu.VMEM((2 * MAIN, WIDTH), BF16),
            pltpu.SemaphoreType.DMA((SEMS,)),
            pltpu.SemaphoreType.DMA((SEMS,)),
            pltpu.SemaphoreType.DMA((6,)),
        ],
        compiler_params=pltpu.CompilerParams(
            collective_id=0, has_side_effects=True, vmem_limit_bytes=44 << 20
        ),
        name="head_step",
    )(teacher_feats.reshape(32, FEAT), student_feats.reshape(2 * MAIN, WIDTH), norm_gain, head_weight.reshape(128, WIDTH), slot_image.transpose(0, 1, 3, 2), slot_count)
    return (
        loss,
        sgrad.reshape(student_feats.shape),
        hgrad.reshape(1, 128, WIDTH),
        gain_grad,
    )


def solution(mesh):
    return jax.shard_map(
        shards,
        mesh=mesh,
        in_specs=(
            P("teacher", ("group", "dp"), None),
            P("group", "teacher", "dp", None, None, None),
            P("group", None),
            P("group", ("teacher", "dp"), None),
            P(None, "teacher", None, None),
            P(None, "teacher", None),
        ),
        out_specs=(
            P("group"),
            P("group", "teacher", "dp", None, None, None),
            P("group", ("teacher", "dp"), None),
            P("group", None),
        ),
        check_vma=False,
    )
```

time: 101 us -> 87.3 us (0.86)
  Pallas kernels: 90.7 us -> 80.4 us
  local copies, waits for them, and re-layouts: 8.4 us -> 4.43 us
  between operations: 0.68 us -> 2.41 us
  other arithmetic: 1.23 us -> 0 us
    pallas_call x1, Pallas kernels: 90.7 us -> 80.4 us  [shards(): pl.pallas_call(kernel, out_shape=(jax.ShapeDtypeStruct((1,), F32), jax.Sh...]
    slice x2 -> x0, local copies, waits for them, and re-layouts: 2.5 us -> none  [the longest x1 1.32 us: shards(): small[0:1]]
    reshape x5 -> x1, local copies, waits for them, and re-layouts: 2.36 us -> 1.07 us  [shards(): teacher_feats.reshape(32, FEAT)]
    unnamed x10 -> x13, local copies, waits for them, and re-layouts: 3.54 us -> 3.35 us
where the time goes in v2:
time: 87.3 us; the launch traced here: 87.2 us
  Pallas kernels  80.4 us (92%)
  local copies, waits for them, and re-layouts  4.43 us (5%)
  between operations  2.41 us (3%)
    pallas_call x1, Pallas kernels, shards(): pl.pallas_call(kernel, out_shape=(jax.ShapeDtypeStruct((1,), F32), jax.Sh...  80.4 us
    unnamed x13, local copies, waits for them, and re-layouts  3.35 us

profile of v2, /device:TPU:1, one launch (start us, length us, event | category | flops | bytes accessed | tf_op | source)
XLA Modules:
  0.0 87.2 jit_solution(3655354498979471601)
XLA Ops:
  0.6 0.0 copy-start.1
  0.6 0.0 copy-start.2
  0.7 0.0 copy-start.3
  0.7 0.0 copy-start.4
  0.7 1.1 %reshape.23.teach = bf16[32,4096]{1,0:T(8,128)(2,1)S(1)} reshape(bf16[8,4,4096]{2,1,0:T(4,128)(2,1)} %param.6) | data formatting | bytes 524288 | tf_op jit(solution)/shard_map/reshape | solution.py:433
  1.8 0.0 copy-done.1
  1.8 0.0 copy-done.2
  1.8 0.0 copy-done.3
  1.8 0.0 copy-done.4
  1.8 0.0 copy-start
  1.8 1.1 %copy-done = bf16[1,1,1,2,256,768]{5,4,3,2,1,0:T(8,128)(2,1)S(1)} copy-done((bf16[1,1,1,2,256,768]{5,4,3,2,1,0:T(8,128)(2,1)S(1)}, bf16[1,1,1,2,256,768]{5,4,3,2,1,0:T(8,128)(2,1)}, u32[]{:S(2)}) %copy-start) | copy-done | bytes 786456
  2.9 80.4 %head_step.1 = (f32[1]{0:T(128)}, f32[1,768]{1,0:T(1,128)S(1)}, bf16[512,768]{1,0:T(8,128)(2,1)S(1)}, f32[128,768]{1,0:T(8,128)S(1)}) custom-call(bf16[32,4096]{1,0:T(8,128)(2,1)S(1)} %reshape.23.teach, bf16[512,768]{1,0:T(8,128)(2,1)S(1)} %bitcast.7, f32[1,768]{1,0:T(1,128)S(1)} %copy-done.4, bf16[128,768]{1,0:T(8,128)(2,1)S(1)} %bitcast.8, ...), custom_call_target="tpu_custom_call" | custom-call | tf_op jit(solution)/shard_map/head_step/pallas_call | solution.py:386
  83.3 0.9 %copy.14 = bf16[1,1,1,2,256,768]{5,4,3,2,1,0:T(8,128)(2,1)} copy(bf16[1,1,1,2,256,768]{5,4,3,2,1,0:T(8,128)(2,1)S(1)} %bitcast.5) | data formatting | bytes 1572864
  84.2 0.7 copy.15
  85.5 0.6 copy.17
Async XLA Ops:
  0.6 1.1 %copy-start.1 = (bf16[1,128,768]{2,1,0:T(8,128)(2,1)S(1)}, bf16[1,128,768]{2,1,0:T(8,128)(2,1)}, u32[]{:S(2)}) copy-start(bf16[1,128,768]{2,1,0:T(8,128)(2,1)} %param.9) | copy-start | bytes 589828
  0.6 1.1 %copy-start.2 = (s32[8,1,8,2]{2,3,1,0:T(2,128)S(1)}, s32[8,1,8,2]{2,3,1,0:T(2,128)}, u32[]{:S(2)}) copy-start(s32[8,1,8,2]{2,3,1,0:T(2,128)} %param.10) | copy-start | bytes 1540
  0.7 1.1 %copy-start.3 = (s32[8,1,8]{2,1,0:T(1,128)S(1)}, s32[8,1,8]{2,1,0:T(1,128)}, u32[]{:S(2)}) copy-start(s32[8,1,8]{2,1,0:T(1,128)} %used_slots.1) | copy-start | bytes 772
  0.7 1.1 %copy-start.4 = (f32[1,768]{1,0:T(1,128)S(1)}, f32[1,768]{1,0:T(1,128)}, u32[]{:S(2)}) copy-start(f32[1,768]{1,0:T(1,128)} %gain.1) | copy-start | bytes 9220
  1.8 1.1 %copy-start = (bf16[1,1,1,2,256,768]{5,4,3,2,1,0:T(8,128)(2,1)S(1)}, bf16[1,1,1,2,256,768]{5,4,3,2,1,0:T(8,128)(2,1)}, u32[]{:S(2)}) copy-start(bf16[1,1,1,2,256,768]{5,4,3,2,1,0:T(8,128)(2,1)} %param.7) | copy-start | bytes 2359300

commit v3 on v2

--- a/solution.py
+++ b/solution.py
@@ -17,7 +17,7 @@
 PART = 32
 GROUP = 640
 TOTAL = 32 * PATCHES
-SEMS = 104
+SEMS = 46
 
 
 def permutation(size, source_of):
@@ -41,7 +41,7 @@
     xhat, rstd, logits, dlogits, sums, cols,
     stat_out, stat_in, tiny_out, tiny_in,
     g_out, g_own, g_in, gz_out, gz_in,
-    d_all, d_out, d_in, e_in, e_all,
+    d_all, d_out, d_in, relay_out, relay_in, e_in, e_all,
     feats_v, send_sem, recv_sem, local_sem,
 ):
     t = lax.axis_index("teacher")
@@ -60,22 +60,26 @@
         }
 
     used = [0]
-    copies = []
-
-    def send(src, dst, to):
+
+    def group(view):
         index = used[0]
         used[0] += 1
+        return (index, view)
+
+    def send(src, dst, to, into, sent=None):
         copy = pltpu.make_async_remote_copy(
-            src_ref=src, dst_ref=dst, send_sem=send_sem.at[index], recv_sem=recv_sem.at[index],
-            device_id=to, device_id_type=MESH,
+            src_ref=src, dst_ref=dst, send_sem=send_sem.at[into[0] if sent is None else sent],
+            recv_sem=recv_sem.at[into[0]], device_id=to, device_id_type=MESH,
         )
         copy.start()
-        copies.append(copy)
+        if sent is None and into[0] not in sent_views:
+            sent_views[into[0]] = into[1]
         return copy
 
-    def arrive(found):
-        for copy in found:
-            copy.wait_recv()
+    sent_views = {}
+
+    def arrive(into):
+        pltpu.make_async_copy(into[1], into[1], recv_sem.at[into[0]]).wait()
 
     barrier = pltpu.get_barrier_semaphore()
     partners = [device(dx=k) for k in (1, 2, 3)] + [device(dy=k) for k in (1, 2, 3)]
@@ -121,16 +125,43 @@
             extra_out[...] = (normed * second).astype(BF16).reshape(2, 4, PART, WIDTH)
     pl.semaphore_wait(barrier, len(partners))
 
-    slices = []
+    slices = group(arrived.at[pl.ds(0, 3)])
     for k in (1, 3, 2):
         for b in range(4):
             columns = columns_of((x + k) % 4, b)
-            slices.append(send(teach.at[:, columns], arrived.at[x, :, pl.ds(b * 256, 256)], device(dx=k)))
-    head_z = send(head, heads.at[mine], device(dz=4))
-    parts = [send(extra_out.at[:, (x + k) % 4], extra_in.at[k - 1], device(dx=k)) for k in (1, 3, 2)]
-    here = rows_b.at[:, :, x]
-    ring = [send(here, here, device(dx=k)) for k in (1, -1)]
-    head_y = [send(head, heads.at[mine], device(dy=k)) for k in (1, 3, 2)]
+            send(teach.at[:, columns], arrived.at[x, :, pl.ds(b * 256, 256)], device(dx=k), slices)
+    head_z = group(head)
+    send(head, heads.at[mine], device(dz=4), head_z)
+    parts = group(extra_in)
+    for k in (1, 3, 2):
+        send(extra_out.at[:, (x + k) % 4], extra_in.at[k - 1], device(dx=k), parts)
+
+    def rows_out(h):
+        here = rows_b.at[h, :, x]
+        into = group(rows_b.at[h, :, pl.ds(0, 2)])
+        for k in (1, -1):
+            send(here, here, device(dx=k), into)
+        return into
+
+    def rows_on(h, found):
+        arrive(found)
+        left, right = rows_b.at[h, pl.ds(0, 2), (x + 3) % 4], rows_b.at[h, pl.ds(2, 2), (x + 1) % 4]
+        into = group(rows_b.at[h, :, 0])
+        send(left, left, device(dx=1), into)
+        send(right, right, device(dx=-1), into)
+        return into
+
+    def tails_out(h):
+        tail = rows_b.at[h, x, 4]
+        into = group(rows_b.at[h, pl.ds(0, 3), 4])
+        for k in (1, 3, 2):
+            send(tail, tail, device(dx=k), into)
+        return into
+
+    rows_a = rows_out(0)
+    head_y = group(heads.at[pl.ds(0, 6)])
+    for k in (1, 3, 2):
+        send(head, heads.at[mine], device(dy=k), head_y)
 
     arrive(slices)
     for copy in owned:
@@ -144,51 +175,60 @@
         h, q = places[step]
         return target[h].at[q, pl.ds(half * 4, 4), core]
 
-    shared = [[], []]
+    shared = [group(target[h].at[:, :, 0]) for h in range(2)]
+    chunks_sent = used[0]
+    used[0] += 1
+    sent_views[chunks_sent] = near_target.at[:, pl.ds(0, 7)]
 
     def pass_on(step, half, ways):
         piece = chunk(step, half)
-        found = [send(piece, chunk(step - way, half), device(dz=way)) for way in ways]
-        shared[places[step][0]].append(send(piece, piece, device(dc=1)))
-        return found
-
-    first = [pass_on(0, half, (1, -1)) for half in range(2)]
-    from_low = [first[0][0], first[1][0]]
-    from_high = [first[0][1], first[1][1]]
-
-    def ring_step(step):
+        found = [send(piece, chunk(step - way, half), device(dz=way), group(piece), chunks_sent) for way in ways]
+        send(piece, piece, device(dc=1), shared[places[step][0]])
+        return found[0] if found else None
+
+    def first_step():
+        up, down = [None, None], [None, None]
+        for half in range(2):
+            up[half] = send(chunk(0, half), chunk(-1, half), device(dz=1), group(chunk(0, half)), chunks_sent)
+            other = 1 - half
+            down[other] = send(chunk(0, other), chunk(1, other), device(dz=-1), group(chunk(0, other)), chunks_sent)
+        for half in range(2):
+            pass_on(0, half, ())
+        return up, down
+
+    from_low, from_high = first_step()
+
+    def ring_step(step, halves=(0, 1)):
         last = step == 3
-        for half in range(2):
+        for half in halves:
             from_low[half].wait_recv()
-            ways = () if last and half == 1 else (1,)
-            found = pass_on(-step, half, ways)
-            from_low[half] = found[0] if found else None
-            from_high[half].wait_recv()
-            ways = () if last and half == 0 else (-1,)
-            found = pass_on(step, half, ways)
-            from_high[half] = found[0] if found else None
+            from_low[half] = pass_on(-step, half, () if last and half == 1 else (1,))
+            other = 1 - half
+            from_high[other].wait_recv()
+            from_high[other] = pass_on(step, other, () if last and other == 0 else (-1,))
 
     arrive(parts)
     quarter = extra_out[:, x].astype(F32)
     quarter += extra_in[0].astype(F32) + extra_in[1].astype(F32) + extra_in[2].astype(F32)
     rows_b[:, x, 4] = quarter.astype(BF16)
-    tail = rows_b.at[:, x, 4]
-    tails = [send(tail, tail, device(dx=k)) for k in (1, 3, 2)]
-
-    head_z.wait_recv()
+    tails_a = tails_out(0)
+    rows_b1 = rows_out(1)
+
+    arrive(head_z)
     theirs = heads.at[t * 2 + 1 - zh]
-    head_y += [send(theirs, theirs, device(dy=k)) for k in (1, 3, 2)]
-
-    ring_step(1)
-
-    arrive(ring)
-    left, right = rows_b.at[0, :, (x + 3) % 4], rows_b.at[1, :, (x + 1) % 4]
-    ring = [send(left, left, device(dx=1)), send(right, right, device(dx=-1))]
-    ring_step(2)
-    ring_step(3)
+    for k in (1, 3, 2):
+        send(theirs, theirs, device(dy=k), head_y)
+
+    ring_step(1, (0,))
+    rows_a = rows_on(0, rows_a)
+    tails_b = tails_out(1)
+    ring_step(1, (1,))
+    ring_step(2, (0,))
+    rows_b1 = rows_on(1, rows_b1)
+    ring_step(2, (1,))
     arrive(head_y)
-    arrive(ring)
-    arrive(tails)
+    arrive(rows_a)
+    arrive(tails_a)
 
     extra_image = jnp.int32(0)
     extra_weight = jnp.float32(0)
@@ -239,8 +279,11 @@
         lax.fori_loop(0, 4, step, 0)
         for k in range(GROUP // 128):
             at = pl.ds(k * 128, 128)
-            stat_out[h, :, at] = jnp.transpose(sums[h, at, :])[:8]
-        return [send(stat_out.at[h], stat_in.at[k - 1, h], device(dx=k)) for k in (1, 3, 2)]
+            stat_out[h, :, at] = jnp.transpose(sums[h, at, :])[:4]
+        into = group(stat_in.at[:, h])
+        for k in (1, 3, 2):
+            send(stat_out.at[h], stat_in.at[k - 1, h], device(dx=k), into)
+        return into
 
     def factors(h):
         total = (stat_out[h] + stat_in[0, h] + stat_in[1, h] + stat_in[2, h]) * (1.0 / FEAT)
@@ -270,39 +313,78 @@
             return carry
 
         lax.fori_loop(0, 2, step, 0)
-        ext = [send(d_out.at[h, (x + k) % 4, 4], e_in.at[k - 1, h], device(dx=k)) for k in (1, 3, 2)]
-        main = [send(d_out.at[h, :, (x + k) % 4], d_in.at[k - 1, h], device(dx=k)) for k in (1, 3, 2)]
-        return ext, main
-
-    def extra_sum(h):
+
+    def send_rows(h):
+        low, high = pl.ds(0, 2), pl.ds(2, 2)
+        across = (x + 2) % 4
+        relay = group(relay_in.at[:, h])
+        send(d_out.at[h, low, across], relay_in.at[0, h], device(dx=1), relay)
+        send(d_out.at[h, high, across], relay_in.at[1, h], device(dx=-1), relay)
+        ext = group(e_in.at[:, h])
+        for k in (1, 3, 2):
+            send(d_out.at[h, (x + k) % 4, 4], e_in.at[k - 1, h], device(dx=k), ext)
+        return relay, ext
+
+    def send_plain(h):
+        low, high = pl.ds(0, 2), pl.ds(2, 2)
+        main = group(d_in.at[:, h])
+        send(d_out.at[h, high, (x + 1) % 4], d_in.at[0, h, high], device(dx=1), main)
+        send(d_out.at[h, low, (x + 3) % 4], d_in.at[1, h, low], device(dx=-1), main)
+        return main
+
+    def relay_on(h, relay, main):
+        low, high = pl.ds(0, 2), pl.ds(2, 2)
+        after, before = (x + 1) % 4, (x + 3) % 4
+        arrive(relay)
+        relay_out[0, h] = (d_all[h, low, after] + relay_in[0, h].astype(F32)).astype(BF16)
+        send(relay_out.at[0, h], d_in.at[0, h, low], device(dx=1), main)
+        relay_out[1, h] = (d_all[h, high, before] + relay_in[1, h].astype(F32)).astype(BF16)
+        send(relay_out.at[1, h], d_in.at[1, h, high], device(dx=-1), main)
+
+    def extra_sum(h, ext):
+        arrive(ext)
         total = d_all[h, x, 4]
         for k in range(3):
             total += e_in[k, h].astype(F32)
         e_all[h, x] = total.astype(BF16)
         piece = e_all.at[h, x]
-        return [send(piece, piece, device(dx=k)) for k in (1, 3, 2)]
+        into = group(e_all.at[h, pl.ds(0, 3)])
+        for k in (1, 3, 2):
+            send(piece, piece, device(dx=k), into)
+        return into
 
     forward(0)
     arrive(shared[0])
     stats_a = statistics(0)
+    ring_step(3, (0,))
+    arrive(rows_b1)
+    arrive(tails_b)
     forward(1)
+    ring_step(3, (1,))
+    arrive(stats_a)
+    loss += factors(0)
+    row_gradient(0)
+    relay_a, ext_a = send_rows(0)
     from_low[0].wait_recv()
     pass_on(-4, 0, ())
     from_high[1].wait_recv()
     pass_on(4, 1, ())
     arrive(shared[1])
     stats_b = statistics(1)
-    arrive(stats_a)
-    loss += factors(0)
-    ext_a, main_a = row_gradient(0)
+    main_a = send_plain(0)
     arrive(stats_b)
     loss += factors(1)
 
+    far, close = (1 - zh) * 128, zh * 128
     gain_part = jnp.zeros((1, WIDTH), F32)
-    away, near = [], []
-    far = pl.ds(pl.multiple_of((1 - zh) * 128, 128), 128)
-    close = pl.ds(pl.multiple_of(zh * 128, 128), 128)
-    for k in (2, 1, 3, 0):
+    away = [group(g_in.at[:, pl.ds(0, 64)]) for _ in range(2)]
+    near = group(g_in.at[:, pl.ds(0, 128)])
+
+    def send_half(k, start, size, into):
+        at = pl.ds(pl.multiple_of(start, 64), size)
+        send(g_out.at[k - 1, at], g_in.at[k - 1, at], device(dy=k), into)
+
+    for k in (1, 3, 2, 0):
         to = (t + k) % 4
         columns = pl.ds(pl.multiple_of(to * 256, 256), 256)
         part = dot(
@@ -312,40 +394,55 @@
         gain_part += jnp.sum(part * head_part, axis=0, keepdims=True)
         if k:
             g_out[k - 1] = part.astype(BF16)
-            away.append(send(g_out.at[k - 1, far], g_in.at[0, k - 1], device(dy=k)))
+            send_half(k, far, 64, away[0])
+            send_half(k, far + 64, 64, away[1])
         else:
             g_own[...] = part
-    for k in (2, 1, 3):
-        near.append(send(g_out.at[k - 1, close], g_in.at[1, k - 1], device(dy=k)))
+        if k == 3:
+            relay_on(0, relay_a, main_a)
+        if k == 2:
+            for other in (1, 3, 2):
+                send_half(other, close, 128, near)
+            row_gradient(1)
+            relay_b, ext_b = send_rows(1)
+            main_b = send_plain(1)
+            ext_all = [extra_sum(0, ext_a)]
 
     which = lax.broadcasted_iota(jnp.int32, (8, WIDTH), 0)
     tiny = jnp.where(which == 0, gain_part / gain[...], jnp.where(which == 1, loss, 0.0))
     tiny_out[0] = tiny
-    tiny_x = [send(tiny_out.at[0], tiny_in.at[k - 1], device(dx=k)) for k in (1, 3, 2)]
-
-    ext_b, main_b = row_gradient(1)
-
+    tiny_z = group(tiny_in.at[6])
+    send(tiny_out.at[0], tiny_in.at[6], device(dz=4), tiny_z)
+
+    def rows_from_y(start, size):
+        at = pl.ds(pl.multiple_of(start, 64), size)
+        part = g_own[at, :]
+        for k in range(3):
+            part += g_in[k, at].astype(F32)
+        return part
+
+    relay_on(1, relay_b, main_b)
+    arrive(tiny_z)
+    tiny += tiny_in[6]
+    tiny_out[1] = tiny
+    tiny_x = group(tiny_in.at[pl.ds(0, 3)])
+    for k in (1, 3, 2):
+        send(tiny_out.at[1], tiny_in.at[k - 1], device(dx=k), tiny_x)
+    across = []
+    for c in range(2):
+        arrive(away[c])
+        at = pl.ds(c * 64, 64)
+        gz_out[at, :] = rows_from_y(far + c * 64, 64).astype(BF16)
+        across.append(group(gz_in.at[at]))
+        send(gz_out.at[at], gz_in.at[at], device(dz=4), across[c])
+        if c == 0:
+            ext_all.append(extra_sum(1, ext_b))
     arrive(tiny_x)
     tiny += tiny_in[0] + tiny_in[1] + tiny_in[2]
-    tiny_out[1] = tiny
-    tiny_z = send(tiny_out.at[1], tiny_in.at[6], device(dz=4))
-
-    arrive(ext_a)
-    ext_all = extra_sum(0)
-    arrive(ext_b)
-    ext_all += extra_sum(1)
-
-    tiny_z.wait_recv()
-    tiny += tiny_in[6]
     tiny_out[2] = tiny
-    tiny_y = [send(tiny_out.at[2], tiny_in.at[2 + k], device(dy=k)) for k in (1, 3, 2)]
-
-    arrive(away)
-    part = g_own[far, :]
-    for k in range(3):
-        part += g_in[0, k].astype(F32)
-    gz_out[...] = part.astype(BF16)
-    across = send(gz_out, gz_in, device(dz=4))
+    tiny_y = group(tiny_in.at[pl.ds(3, 3)])
+    for k in (1, 3, 2):
+        send(tiny_out.at[2], tiny_in.at[2 + k], device(dy=k), tiny_y)
 
     def finish(dnormed, part):
         dx = dnormed.reshape(MAIN, WIDTH) * gain[...]
@@ -355,28 +452,23 @@
         out = (rstd[part, :][:, 0:1] * (dx - drop - unit * along)).astype(BF16)
         sgrad_o[part, :] = dot(order, out, ((0,), (0,))).astype(BF16)
 
-    arrive(ext_all)
-    finish(e_all[...].astype(F32) * second, pl.ds(MAIN, MAIN))
-
     arrive(main_a)
     arrive(main_b)
-    dn = d_all[:, :, x]
-    for k in range(3):
-        dn += d_in[k].astype(F32)
-    finish(dn, pl.ds(0, MAIN))
-
+    finish(d_all[:, :, x] + d_in[0].astype(F32) + d_in[1].astype(F32), pl.ds(0, MAIN))
+    arrive(ext_all[0])
+    arrive(ext_all[1])
+    finish(e_all[...].astype(F32) * second, pl.ds(MAIN, MAIN))
     arrive(near)
-    part = g_own[close, :]
-    for k in range(3):
-        part += g_in[1, k].astype(F32)
-    across.wait_recv()
-    hgrad_o[...] = part + gz_in[...].astype(F32)
+    hgrad_o[...] = rows_from_y(close, 128)
+    arrive(across[0])
+    arrive(across[1])
+    hgrad_o[...] += gz_in[...].astype(F32)
     arrive(tiny_y)
     tiny += tiny_in[3] + tiny_in[4] + tiny_in[5]
     gain_o[...] = tiny[0:1]
     loss_o[0] = tiny[1, 0]
-    for copy in copies:
-        copy.wait_send()
+    for index, view in sent_views.items():
+        pltpu.make_async_copy(view, view, send_sem.at[index]).wait()
 
 
 def shards(teacher_feats, student_feats, norm_gain, head_weight, slot_image, slot_count):
@@ -387,7 +479,7 @@
         kernel,
         out_shape=(
             jax.ShapeDtypeStruct((1,), F32),
-            jax.ShapeDtypeStruct((1, WIDTH), F32),
+            pltpu.VMEM((1, WIDTH), F32),
             pltpu.VMEM((2 * MAIN, WIDTH), BF16),
             pltpu.VMEM((128, WIDTH), F32),
         ),
@@ -407,18 +499,20 @@
             pltpu.VMEM((2, 4, 160, SLICE), BF16),
             pltpu.VMEM((2, GROUP, 128), F32),
             pltpu.VMEM((2, GROUP, 128), F32),
-            pltpu.VMEM((2, 8, GROUP), F32),
-            pltpu.VMEM((3, 2, 8, GROUP), F32),
+            pltpu.VMEM((2, 4, GROUP), F32),
+            pltpu.VMEM((3, 2, 4, GROUP), F32),
             pltpu.VMEM((3, 8, WIDTH), F32),
             pltpu.VMEM((7, 8, WIDTH), F32),
             pltpu.VMEM((3, 256, WIDTH), BF16),
             pltpu.VMEM((256, WIDTH), F32),
-            pltpu.VMEM((2, 3, 128, WIDTH), BF16),
+            pltpu.VMEM((3, 256, WIDTH), BF16),
             pltpu.VMEM((128, WIDTH), BF16),
             pltpu.VMEM((128, WIDTH), BF16),
             pltpu.VMEM((2, 4, 5, PART, WIDTH), F32),
             pltpu.VMEM((2, 4, 5, PART, WIDTH), BF16),
-            pltpu.VMEM((3, 2, 4, PART, WIDTH), BF16),
+            pltpu.VMEM((2, 2, 4, PART, WIDTH), BF16),
+            pltpu.VMEM((2, 2, 2, PART, WIDTH), BF16),
+            pltpu.VMEM((2, 2, 2, PART, WIDTH), BF16),
             pltpu.VMEM((3, 2, PART, WIDTH), BF16),
             pltpu.VMEM((2, 4, PART, WIDTH), BF16),
             pltpu.VMEM((2 * MAIN, WIDTH), BF16),

time: 87.3 us -> 79.3 us (0.908)
  Pallas kernels: 80.4 us -> 72.1 us
    pallas_call x1, Pallas kernels: 80.4 us -> 72.1 us  [shards(): pl.pallas_call(kernel, out_shape=(jax.ShapeDtypeStruct((1,), F32), pltpu....]
where the time goes in v3:
time: 79.3 us; the launch traced here: 79 us
  Pallas kernels  72.1 us (91%)
  local copies, waits for them, and re-layouts  4.42 us (6%)
  between operations  2.41 us (3%)
    pallas_call x1, Pallas kernels, shards(): pl.pallas_call(kernel, out_shape=(jax.ShapeDtypeStruct((1,), F32), pltpu....  72.1 us
    unnamed x13, local copies, waits for them, and re-layouts  3.35 us

profile of v3, /device:TPU:1, one launch (start us, length us, event | category | flops | bytes accessed | tf_op | source)
XLA Modules:
  0.0 79.0 jit_solution(16514291699329191612)
XLA Ops:
  0.6 0.0 copy-start.1
  0.6 0.0 copy-start.2
  0.7 0.0 copy-start.3
  0.7 0.0 copy-start.4
  0.7 1.1 %reshape.23.teach = bf16[32,4096]{1,0:T(8,128)(2,1)S(1)} reshape(bf16[8,4,4096]{2,1,0:T(4,128)(2,1)} %param.6) | data formatting | bytes 524288 | tf_op jit(solution)/shard_map/reshape | solution.py:527
  1.8 0.0 copy-done.1
  1.8 0.0 copy-done.2
  1.8 0.0 copy-done.3
  1.8 0.0 copy-done.4
  1.8 0.0 copy-start
  1.8 1.1 %copy-done = bf16[1,1,1,2,256,768]{5,4,3,2,1,0:T(8,128)(2,1)S(1)} copy-done((bf16[1,1,1,2,256,768]{5,4,3,2,1,0:T(8,128)(2,1)S(1)}, bf16[1,1,1,2,256,768]{5,4,3,2,1,0:T(8,128)(2,1)}, u32[]{:S(2)}) %copy-start) | copy-done | bytes 786456
  2.9 72.1 %head_step.1 = (f32[1]{0:T(128)}, f32[1,768]{1,0:T(1,128)S(1)}, bf16[512,768]{1,0:T(8,128)(2,1)S(1)}, f32[128,768]{1,0:T(8,128)S(1)}) custom-call(bf16[32,4096]{1,0:T(8,128)(2,1)S(1)} %reshape.23.teach, bf16[512,768]{1,0:T(8,128)(2,1)S(1)} %bitcast.7, f32[1,768]{1,0:T(1,128)S(1)} %copy-done.4, bf16[128,768]{1,0:T(8,128)(2,1)S(1)} %bitcast.8, ...), custom_call_target="tpu_custom_call" | custom-call | tf_op jit(solution)/shard_map/head_step/pallas_call | solution.py:478
  75.1 0.9 %copy.14 = bf16[1,1,1,2,256,768]{5,4,3,2,1,0:T(8,128)(2,1)} copy(bf16[1,1,1,2,256,768]{5,4,3,2,1,0:T(8,128)(2,1)S(1)} %bitcast.5) | data formatting | bytes 1572864
  76.0 0.7 copy.15
  76.7 0.6 copy.16
Async XLA Ops:
  0.6 1.1 %copy-start.1 = (bf16[1,128,768]{2,1,0:T(8,128)(2,1)S(1)}, bf16[1,128,768]{2,1,0:T(8,128)(2,1)}, u32[]{:S(2)}) copy-start(bf16[1,128,768]{2,1,0:T(8,128)(2,1)} %param.9) | copy-start | bytes 589828
  0.6 1.1 %copy-start.2 = (s32[8,1,8,2]{2,3,1,0:T(2,128)S(1)}, s32[8,1,8,2]{2,3,1,0:T(2,128)}, u32[]{:S(2)}) copy-start(s32[8,1,8,2]{2,3,1,0:T(2,128)} %param.10) | copy-start | bytes 1540
  0.7 1.1 %copy-start.3 = (s32[8,1,8]{2,1,0:T(1,128)S(1)}, s32[8,1,8]{2,1,0:T(1,128)}, u32[]{:S(2)}) copy-start(s32[8,1,8]{2,1,0:T(1,128)} %used_slots.1) | copy-start | bytes 772
  0.7 1.1 %copy-start.4 = (f32[1,768]{1,0:T(1,128)S(1)}, f32[1,768]{1,0:T(1,128)}, u32[]{:S(2)}) copy-start(f32[1,768]{1,0:T(1,128)} %gain.1) | copy-start | bytes 9220
  1.8 1.1 %copy-start = (bf16[1,1,1,2,256,768]{5,4,3,2,1,0:T(8,128)(2,1)S(1)}, bf16[1,1,1,2,256,768]{5,4,3,2,1,0:T(8,128)(2,1)}, u32[]{:S(2)}) copy-start(bf16[1,1,1,2,256,768]{5,4,3,2,1,0:T(8,128)(2,1)} %param.7) | copy-start | bytes 2359300

commit v4 on v3

--- a/solution.py
+++ b/solution.py
@@ -17,7 +17,7 @@
 PART = 32
 GROUP = 640
 TOTAL = 32 * PATCHES
-SEMS = 46
+RECV_SEMS, SEND_SEMS = 45, 32
 
 
 def permutation(size, source_of):
@@ -35,14 +35,14 @@
 
 
 def kernel(
-    teach, feats, gain, head, images, used_slots,
+    teach, feats, gain_h, head, images_h, used_slots_h,
     loss_o, gain_o, sgrad_o, hgrad_o,
     arrived, near_target, far_target, heads, rows_b, extra_out, extra_in,
     xhat, rstd, logits, dlogits, sums, cols,
-    stat_out, stat_in, tiny_out, tiny_in,
-    g_out, g_own, g_in, gz_out, gz_in,
+    stat_out, stat_in, tiny_out, tiny_in, g_near,
+    g_out, g_own, g_in, y_relay, y_sum, n_in, gz_out, gz_in,
     d_all, d_out, d_in, relay_out, relay_in, e_in, e_all,
-    feats_v, send_sem, recv_sem, local_sem,
+    feats_v, gain, images, used_slots, send_sem, recv_sem, local_sem,
 ):
     t = lax.axis_index("teacher")
     g = lax.axis_index("group")
@@ -59,7 +59,7 @@
             "dp": ((x + dx + 4) % 4) * 2 + to_z // 4,
         }
 
-    used = [0]
+    used = [0, 0]
 
     def group(view):
         index = used[0]
@@ -67,16 +67,20 @@
         return (index, view)
 
     def send(src, dst, to, into, sent=None):
+        if sent is None:
+            if into[0] not in sent_by:
+                sent_by[into[0]] = used[1]
+                sent_views[used[1]] = into[1]
+                used[1] += 1
+            sent = sent_by[into[0]]
         copy = pltpu.make_async_remote_copy(
-            src_ref=src, dst_ref=dst, send_sem=send_sem.at[into[0] if sent is None else sent],
+            src_ref=src, dst_ref=dst, send_sem=send_sem.at[sent],
             recv_sem=recv_sem.at[into[0]], device_id=to, device_id_type=MESH,
         )
         copy.start()
-        if sent is None and into[0] not in sent_views:
-            sent_views[into[0]] = into[1]
         return copy
 
-    sent_views = {}
+    sent_by, sent_views = {}, {}
 
     def arrive(into):
         pltpu.make_async_copy(into[1], into[1], recv_sem.at[into[0]]).wait()
@@ -94,8 +98,12 @@
         return (at % 4) * 64 + c * 32 + xs * 8 + (at // 4) * 4 + p
 
     mine = t * 2 + zh
-    feats_in = pltpu.make_async_copy(feats, feats_v, local_sem.at[0])
-    feats_in.start()
+    inputs = [
+        pltpu.make_async_copy(src, dst, local_sem.at[6 + n])
+        for n, (src, dst) in enumerate(((images_h, images), (used_slots_h, used_slots), (gain_h, gain), (feats, feats_v)))
+    ]
+    for copy in inputs:
+        copy.start()
 
     def columns_of(to, b):
         return pl.ds(pl.multiple_of(b * SLICE + to * 256, 256), 256)
@@ -103,11 +111,12 @@
     owned = [pltpu.make_async_copy(head, heads.at[mine], local_sem.at[1])]
     for b in range(4):
         owned.append(pltpu.make_async_copy(
-            teach.at[:, columns_of(x, b)], arrived.at[x, :, pl.ds(b * 256, 256)], local_sem.at[2 + b]
+            teach.at[:, :, columns_of(x, b)], arrived.at[x, :, :, pl.ds(b * 256, 256)], local_sem.at[2 + b]
         ))
     for copy in owned:
         copy.start()
-    feats_in.wait()
+    for copy in inputs:
+        copy.wait()
     second = jnp.where(used_slots[g, 0, d] >= 2, 1.0, 0.0).astype(F32)
     order = permutation(MAIN, patch_order)
     for slot in range(2):
@@ -129,9 +138,12 @@
     for k in (1, 3, 2):
         for b in range(4):
             columns = columns_of((x + k) % 4, b)
-            send(teach.at[:, columns], arrived.at[x, :, pl.ds(b * 256, 256)], device(dx=k), slices)
+            send(teach.at[:, :, columns], arrived.at[x, :, :, pl.ds(b * 256, 256)], device(dx=k), slices)
     head_z = group(head)
     send(head, heads.at[mine], device(dz=4), head_z)
+    head_y = group(heads.at[pl.ds(0, 6)])
+    for k in (1, 3, 2):
+        send(head, heads.at[mine], device(dy=k), head_y)
     parts = group(extra_in)
     for k in (1, 3, 2):
         send(extra_out.at[:, (x + k) % 4], extra_in.at[k - 1], device(dx=k), parts)
@@ -159,14 +171,11 @@
         return into
 
     rows_a = rows_out(0)
-    head_y = group(heads.at[pl.ds(0, 6)])
-    for k in (1, 3, 2):
-        send(head, heads.at[mine], device(dy=k), head_y)
 
     arrive(slices)
     for copy in owned:
         copy.wait()
-    own = dot(permutation(128, image_order), arrived[...].reshape(128, SLICE), ((1,), (0,)))
+    own = dot(permutation(128, image_order), arrived[...].astype(F32).reshape(128, SLICE).astype(BF16), ((1,), (0,)))
     target = (near_target, far_target)
     near_target[0, :, core] = own.astype(BF16).reshape(8, 16, SLICE)
     places = {0: (0, 0), -1: (0, 1), 1: (0, 2), -2: (0, 3), 4: (1, 0), -4: (1, 0), 3: (1, 1), -3: (1, 2), 2: (1, 3)}
@@ -176,8 +185,8 @@
         return target[h].at[q, pl.ds(half * 4, 4), core]
 
     shared = [group(target[h].at[:, :, 0]) for h in range(2)]
-    chunks_sent = used[0]
-    used[0] += 1
+    chunks_sent = used[1]
+    used[1] += 1
     sent_views[chunks_sent] = near_target.at[:, pl.ds(0, 7)]
 
     def pass_on(step, half, ways):
@@ -320,10 +329,13 @@
         relay = group(relay_in.at[:, h])
         send(d_out.at[h, low, across], relay_in.at[0, h], device(dx=1), relay)
         send(d_out.at[h, high, across], relay_in.at[1, h], device(dx=-1), relay)
+        return relay
+
+    def send_extra(h):
         ext = group(e_in.at[:, h])
         for k in (1, 3, 2):
             send(d_out.at[h, (x + k) % 4, 4], e_in.at[k - 1, h], device(dx=k), ext)
-        return relay, ext
+        return ext
 
     def send_plain(h):
         low, high = pl.ds(0, 2), pl.ds(2, 2)
@@ -363,14 +375,25 @@
     ring_step(3, (1,))
     arrive(stats_a)
     loss += factors(0)
-    row_gradient(0)
-    relay_a, ext_a = send_rows(0)
     from_low[0].wait_recv()
     pass_on(-4, 0, ())
     from_high[1].wait_recv()
     pass_on(4, 1, ())
+    row_gradient(0)
+    relay_a = send_rows(0)
     arrive(shared[1])
     stats_b = statistics(1)
+
+    def head_part(h, columns):
+        lhs = dlogits[h, :, :, columns].reshape(GROUP, 256)
+        return dot(lhs, rows_b[h].reshape(GROUP, WIDTH), ((0,), (0,)))
+
+    def columns_for(k):
+        return pl.ds(pl.multiple_of((t + k) % 4 * 256, 256), 256)
+
+    for k in (1, 3, 2, 0):
+        g_near[k] = head_part(0, columns_for(k))
+    ext_a = send_extra(0)
     main_a = send_plain(0)
     arrive(stats_b)
     loss += factors(1)
@@ -378,7 +401,8 @@
     far, close = (1 - zh) * 128, zh * 128
     gain_part = jnp.zeros((1, WIDTH), F32)
     away = [group(g_in.at[:, pl.ds(0, 64)]) for _ in range(2)]
-    near = group(g_in.at[:, pl.ds(0, 128)])
+    near = group(n_in)
+    turned = group(y_relay)
 
     def send_half(k, start, size, into):
         at = pl.ds(pl.multiple_of(start, 64), size)
@@ -386,34 +410,36 @@
 
     for k in (1, 3, 2, 0):
         to = (t + k) % 4
-        columns = pl.ds(pl.multiple_of(to * 256, 256), 256)
-        part = dot(
-            dlogits[:, :, :, columns].reshape(2 * GROUP, 256), rows_b[...].reshape(2 * GROUP, WIDTH), ((0,), (0,))
-        )
-        head_part = heads[pl.ds(to * 2, 2)].reshape(256, WIDTH).astype(F32)
-        gain_part += jnp.sum(part * head_part, axis=0, keepdims=True)
+        part = g_near[k] + head_part(1, columns_for(k))
+        weights = heads[pl.ds(to * 2, 2)].reshape(256, WIDTH).astype(F32)
+        gain_part += jnp.sum(part * weights, axis=0, keepdims=True)
         if k:
             g_out[k - 1] = part.astype(BF16)
             send_half(k, far, 64, away[0])
             send_half(k, far + 64, 64, away[1])
+            g_near[k] = part
         else:
             g_own[...] = part
         if k == 3:
             relay_on(0, relay_a, main_a)
-        if k == 2:
-            for other in (1, 3, 2):
-                send_half(other, close, 128, near)
-            row_gradient(1)
-            relay_b, ext_b = send_rows(1)
-            main_b = send_plain(1)
-            ext_all = [extra_sum(0, ext_a)]
-
-    which = lax.broadcasted_iota(jnp.int32, (8, WIDTH), 0)
-    tiny = jnp.where(which == 0, gain_part / gain[...], jnp.where(which == 1, loss, 0.0))
+
+    which = lax.broadcasted_iota(jnp.int32, (2, WIDTH), 0)
+    tiny = jnp.where(which == 0, gain_part / gain[...], loss)
     tiny_out[0] = tiny
-    tiny_z = group(tiny_in.at[6])
-    send(tiny_out.at[0], tiny_in.at[6], device(dz=4), tiny_z)
-
+    tiny_x = group(tiny_in.at[pl.ds(0, 3)])
+    for k in (1, 3, 2):
+        send(tiny_out.at[0], tiny_in.at[k - 1], device(dx=k), tiny_x)
+    row_gradient(1)
+    relay_b = send_rows(1)
+    ext_b = send_extra(1)
+    main_b = send_plain(1)
+    ext_all = [extra_sum(0, ext_a)]
+    arrive(tiny_x)
+    tiny += tiny_in[0] + tiny_in[1] + tiny_in[2]
+    tiny_out[1] = tiny
+    tiny_y = group(tiny_in.at[pl.ds(3, 3)])
+    for k in (1, 3, 2):
+        send(tiny_out.at[1], tiny_in.at[2 + k], device(dy=k), tiny_y)
     def rows_from_y(start, size):
         at = pl.ds(pl.multiple_of(start, 64), size)
         part = g_own[at, :]
@@ -422,12 +448,6 @@
         return part
 
     relay_on(1, relay_b, main_b)
-    arrive(tiny_z)
-    tiny += tiny_in[6]
-    tiny_out[1] = tiny
-    tiny_x = group(tiny_in.at[pl.ds(0, 3)])
-    for k in (1, 3, 2):
-        send(tiny_out.at[1], tiny_in.at[k - 1], device(dx=k), tiny_x)
     across = []
     for c in range(2):
         arrive(away[c])
@@ -436,13 +456,26 @@
         across.append(group(gz_in.at[at]))
         send(gz_out.at[at], gz_in.at[at], device(dz=4), across[c])
         if c == 0:
-            ext_all.append(extra_sum(1, ext_b))
-    arrive(tiny_x)
-    tiny += tiny_in[0] + tiny_in[1] + tiny_in[2]
+            at = pl.ds(pl.multiple_of(close, 64), 64)
+            send(g_out.at[1, at], y_relay.at[0], device(dy=1), turned)
+            at = pl.ds(pl.multiple_of(close + 64, 64), 64)
+            send(g_out.at[1, at], y_relay.at[1], device(dy=-1), turned)
+            send(g_out.at[0, at], n_in.at[0, pl.ds(64, 64)], device(dy=1), near)
+            at = pl.ds(pl.multiple_of(close, 64), 64)
+            send(g_out.at[2, at], n_in.at[1, pl.ds(0, 64)], device(dy=-1), near)
+    ext_all.append(extra_sum(1, ext_b))
+    arrive(turned)
+    at = pl.ds(pl.multiple_of(close, 64), 64)
+    y_sum[0] = (g_near[1, at, :] + y_relay[0].astype(F32)).astype(BF16)
+    send(y_sum.at[0], n_in.at[0, pl.ds(0, 64)], device(dy=1), near)
+    at = pl.ds(pl.multiple_of(close + 64, 64), 64)
+    y_sum[1] = (g_near[3, at, :] + y_relay[1].astype(F32)).astype(BF16)
+    send(y_sum.at[1], n_in.at[1, pl.ds(64, 64)], device(dy=-1), near)
+    arrive(tiny_y)
+    tiny += tiny_in[3] + tiny_in[4] + tiny_in[5]
     tiny_out[2] = tiny
-    tiny_y = group(tiny_in.at[pl.ds(3, 3)])
-    for k in (1, 3, 2):
-        send(tiny_out.at[2], tiny_in.at[2 + k], device(dy=k), tiny_y)
+    tiny_z = group(tiny_in.at[6])
+    send(tiny_out.at[2], tiny_in.at[6], device(dz=4), tiny_z)
 
     def finish(dnormed, part):
         dx = dnormed.reshape(MAIN, WIDTH) * gain[...]
@@ -459,14 +492,15 @@
     arrive(ext_all[1])
     finish(e_all[...].astype(F32) * second, pl.ds(MAIN, MAIN))
     arrive(near)
-    hgrad_o[...] = rows_from_y(close, 128)
+    hgrad_o[...] = g_own[pl.ds(pl.multiple_of(close, 64), 128), :] + n_in[0].astype(F32) + n_in[1].astype(F32)
     arrive(across[0])
     arrive(across[1])
     hgrad_o[...] += gz_in[...].astype(F32)
-    arrive(tiny_y)
-    tiny += tiny_in[3] + tiny_in[4] + tiny_in[5]
+    arrive(tiny_z)
+    tiny += tiny_in[6]
     gain_o[...] = tiny[0:1]
     loss_o[0] = tiny[1, 0]
+    assert used == [RECV_SEMS, SEND_SEMS], used
     for index, view in sent_views.items():
         pltpu.make_async_copy(view, view, send_sem.at[index]).wait()
 
@@ -475,6 +509,10 @@
     vmem = pl.BlockSpec(memory_space=pltpu.VMEM)
     smem = pl.BlockSpec(memory_space=pltpu.SMEM)
     anywhere = pl.BlockSpec(memory_space=pl.ANY)
+    operands = (
+        teacher_feats, student_feats.reshape(2 * MAIN, WIDTH), norm_gain, head_weight.reshape(128, WIDTH),
+        slot_image.transpose(0, 1, 3, 2), slot_count,
+    )
     loss, gain_grad, sgrad, hgrad = pl.pallas_call(
         kernel,
         out_shape=(
@@ -483,10 +521,10 @@
             pltpu.VMEM((2 * MAIN, WIDTH), BF16),
             pltpu.VMEM((128, WIDTH), F32),
         ),
-        in_specs=[anywhere, anywhere, vmem, anywhere, smem, smem],
+        in_specs=[anywhere] * 6,
         out_specs=(smem, vmem, vmem, vmem),
         scratch_shapes=[
-            pltpu.VMEM((4, 32, SLICE), BF16),
+            pltpu.VMEM((4, 8, 4, SLICE), BF16),
             pltpu.VMEM((4, 8, 2, 16, SLICE), BF16),
             pltpu.VMEM((4, 8, 2, 16, SLICE), BF16),
             pltpu.VMEM((8, 128, WIDTH), BF16),
@@ -501,11 +539,15 @@
             pltpu.VMEM((2, GROUP, 128), F32),
             pltpu.VMEM((2, 4, GROUP), F32),
             pltpu.VMEM((3, 2, 4, GROUP), F32),
-            pltpu.VMEM((3, 8, WIDTH), F32),
-            pltpu.VMEM((7, 8, WIDTH), F32),
+            pltpu.VMEM((3, 2, WIDTH), F32),
+            pltpu.VMEM((7, 2, WIDTH), F32),
+            pltpu.VMEM((4, 256, WIDTH), F32),
             pltpu.VMEM((3, 256, WIDTH), BF16),
             pltpu.VMEM((256, WIDTH), F32),
             pltpu.VMEM((3, 256, WIDTH), BF16),
+            pltpu.VMEM((2, 64, WIDTH), BF16),
+            pltpu.VMEM((2, 64, WIDTH), BF16),
+            pltpu.VMEM((2, 128, WIDTH), BF16),
             pltpu.VMEM((128, WIDTH), BF16),
             pltpu.VMEM((128, WIDTH), BF16),
             pltpu.VMEM((2, 4, 5, PART, WIDTH), F32),
@@ -516,15 +558,18 @@
             pltpu.VMEM((3, 2, PART, WIDTH), BF16),
             pltpu.VMEM((2, 4, PART, WIDTH), BF16),
             pltpu.VMEM((2 * MAIN, WIDTH), BF16),
-            pltpu.SemaphoreType.DMA((SEMS,)),
-            pltpu.SemaphoreType.DMA((SEMS,)),
-            pltpu.SemaphoreType.DMA((6,)),
+            pltpu.VMEM((1, WIDTH), F32),
+            pltpu.SMEM((8, 1, 2, 8), jnp.int32),
+            pltpu.SMEM((8, 1, 8), jnp.int32),
+            pltpu.SemaphoreType.DMA((SEND_SEMS,)),
+            pltpu.SemaphoreType.DMA((RECV_SEMS,)),
+            pltpu.SemaphoreType.DMA((10,)),
         ],
         compiler_params=pltpu.CompilerParams(
             collective_id=0, has_side_effects=True, vmem_limit_bytes=44 << 20
         ),
         name="head_step",
-    )(teacher_feats.reshape(32, FEAT), student_feats.reshape(2 * MAIN, WIDTH), norm_gain, head_weight.reshape(128, WIDTH), slot_image.transpose(0, 1, 3, 2), slot_count)
+    )(*[pltpu.with_memory_space_constraint(operand, pltpu.HBM) for operand in operands])
     return (
         loss,
         sgrad.reshape(student_feats.shape),

time: 79.3 us -> 73.2 us (0.923); the launches traced: 79 us -> 72 us
  Pallas kernels: 72.1 us -> 67.5 us
  local copies, waits for them, and re-layouts: 4.42 us -> 2.2 us
    pallas_call x1, Pallas kernels: 72.1 us -> 67.5 us  [shards(): pl.pallas_call(kernel, out_shape=(jax.ShapeDtypeStruct((1,), F32), pltpu....]
    unnamed x13 -> x3, local copies, waits for them, and re-layouts: 3.35 us -> 2.2 us
    reshape x1 -> x0, local copies, waits for them, and re-layouts: 1.07 us -> none  [shards(): teacher_feats.reshape(32, FEAT)]
where the time goes in v4:
time: 73.2 us; the launch traced here: 72 us
  Pallas kernels  67.5 us (92%)
  between operations  2.33 us (3%)
  local copies, waits for them, and re-layouts  2.2 us (3%)
    pallas_call x1, Pallas kernels, shards(): pl.pallas_call(kernel, out_shape=(jax.ShapeDtypeStruct((1,), F32), pltpu....  67.5 us
    unnamed x3, local copies, waits for them, and re-layouts  2.2 us

profile of v4, /device:TPU:1, one launch (start us, length us, event | category | flops | bytes accessed | tf_op | source)
XLA Modules:
  0.0 72.0 jit_solution(15684292658230077866)
XLA Ops:
  0.6 67.5 %head_step.1 = (f32[1]{0:T(128)}, f32[1,768]{1,0:T(1,128)S(1)}, bf16[512,768]{1,0:T(8,128)(2,1)S(1)}, f32[128,768]{1,0:T(8,128)S(1)}) custom-call(bf16[8,4,4096]{2,1,0:T(4,128)(2,1)} %teach.1, bf16[512,768]{1,0:T(8,128)(2,1)} %bitcast.7, f32[1,768]{1,0:T(1,128)} %gain_h.1, bf16[128,768]{1,0:T(8,128)(2,1)} %bitcast.8, s32[8,1,2,8]{3,2,1,0:T(2,128)} %bitcast.9, ...), custom_call_target="tpu_custom_call" | custom-call | tf_op jit(solution)/shard_map/head_step/pallas_call | solution.py:516
  68.1 0.9 %copy.14 = bf16[1,1,1,2,256,768]{5,4,3,2,1,0:T(8,128)(2,1)} copy(bf16[1,1,1,2,256,768]{5,4,3,2,1,0:T(8,128)(2,1)S(1)} %bitcast.5) | data formatting | bytes 1572864
  69.0 0.7 %copy.15 = f32[1,128,768]{2,1,0:T(8,128)} copy(f32[1,128,768]{2,1,0:T(8,128)S(1)} %bitcast.6) | data formatting | bytes 786432
  69.8 0.6 copy.16

commit v5 on v4

--- a/solution.py
+++ b/solution.py
@@ -99,7 +99,7 @@
 
     mine = t * 2 + zh
     inputs = [
-        pltpu.make_async_copy(src, dst, local_sem.at[6 + n])
+        pltpu.make_async_copy(src, dst, local_sem.at[3 + n])
         for n, (src, dst) in enumerate(((images_h, images), (used_slots_h, used_slots), (gain_h, gain), (feats, feats_v)))
     ]
     for copy in inputs:
@@ -109,12 +109,16 @@
         return pl.ds(pl.multiple_of(b * SLICE + to * 256, 256), 256)
 
     owned = [pltpu.make_async_copy(head, heads.at[mine], local_sem.at[1])]
-    for b in range(4):
-        owned.append(pltpu.make_async_copy(
-            teach.at[:, :, columns_of(x, b)], arrived.at[x, :, :, pl.ds(b * 256, 256)], local_sem.at[2 + b]
-        ))
-    for copy in owned:
+    own_columns = [
+        pltpu.make_async_copy(
+            teach.at[:, :, columns_of(x, b)], arrived.at[x, :, :, pl.ds(b * 256, 256)], local_sem.at[2]
+        )
+        for b in range(4)
+    ]
+    for copy in own_columns:
         copy.start()
+    owned.append(pltpu.make_async_copy(arrived.at[x], arrived.at[x], local_sem.at[2]))
+    owned[0].start()
     for copy in inputs:
         copy.wait()
     second = jnp.where(used_slots[g, 0, d] >= 2, 1.0, 0.0).astype(F32)
@@ -408,7 +412,7 @@
         at = pl.ds(pl.multiple_of(start, 64), size)
         send(g_out.at[k - 1, at], g_in.at[k - 1, at], device(dy=k), into)
 
-    for k in (1, 3, 2, 0):
+    for k in (2, 1, 3, 0):
         to = (t + k) % 4
         part = g_near[k] + head_part(1, columns_for(k))
         weights = heads[pl.ds(to * 2, 2)].reshape(256, WIDTH).astype(F32)
@@ -416,11 +420,12 @@
         if k:
             g_out[k - 1] = part.astype(BF16)
             send_half(k, far, 64, away[0])
-            send_half(k, far + 64, 64, away[1])
             g_near[k] = part
         else:
             g_own[...] = part
         if k == 3:
+            for other in (2, 1, 3):
+                send_half(other, far + 64, 64, away[1])
             relay_on(0, relay_a, main_a)
 
     which = lax.broadcasted_iota(jnp.int32, (2, WIDTH), 0)
@@ -433,7 +438,6 @@
     relay_b = send_rows(1)
     ext_b = send_extra(1)
     main_b = send_plain(1)
-    ext_all = [extra_sum(0, ext_a)]
     arrive(tiny_x)
     tiny += tiny_in[0] + tiny_in[1] + tiny_in[2]
     tiny_out[1] = tiny
@@ -448,6 +452,7 @@
         return part
 
     relay_on(1, relay_b, main_b)
+    ext_all = [extra_sum(0, ext_a)]
     across = []
     for c in range(2):
         arrive(away[c])
@@ -563,7 +568,7 @@
             pltpu.SMEM((8, 1, 8), jnp.int32),
             pltpu.SemaphoreType.DMA((SEND_SEMS,)),
             pltpu.SemaphoreType.DMA((RECV_SEMS,)),
-            pltpu.SemaphoreType.DMA((10,)),
+            pltpu.SemaphoreType.DMA((7,)),
         ],
         compiler_params=pltpu.CompilerParams(
             collective_id=0, has_side_effects=True, vmem_limit_bytes=44 << 20

time: 73.2 us -> 72.9 us (level); the launches traced: 72 us -> 72.6 us
  no operation moved by 1% of the time
where the time goes in v5:
time: 72.9 us; the launch traced here: 72.6 us
  Pallas kernels  68 us (93%)
  between operations  2.33 us (3%)
  local copies, waits for them, and re-layouts  2.2 us (3%)
    pallas_call x1, Pallas kernels, shards(): pl.pallas_call(kernel, out_shape=(jax.ShapeDtypeStruct((1,), F32), pltpu....  68 us
    unnamed x3, local copies, waits for them, and re-layouts  2.2 us

profile of v5, /device:TPU:1, one launch (start us, length us, event | category | flops | bytes accessed | tf_op | source)
XLA Modules:
  0.0 72.6 jit_solution(14171516477806310999)
XLA Ops:
  0.6 68.0 %head_step.1 = (f32[1]{0:T(128)}, f32[1,768]{1,0:T(1,128)S(1)}, bf16[512,768]{1,0:T(8,128)(2,1)S(1)}, f32[128,768]{1,0:T(8,128)S(1)}) custom-call(bf16[8,4,4096]{2,1,0:T(4,128)(2,1)} %teach.1, bf16[512,768]{1,0:T(8,128)(2,1)} %bitcast.7, f32[1,768]{1,0:T(1,128)} %gain_h.1, bf16[128,768]{1,0:T(8,128)(2,1)} %bitcast.8, s32[8,1,2,8]{3,2,1,0:T(2,128)} %bitcast.9, ...), custom_call_target="tpu_custom_call" | custom-call | tf_op jit(solution)/shard_map/head_step/pallas_call | solution.py:521
  68.7 0.9 %copy.14 = bf16[1,1,1,2,256,768]{5,4,3,2,1,0:T(8,128)(2,1)} copy(bf16[1,1,1,2,256,768]{5,4,3,2,1,0:T(8,128)(2,1)S(1)} %bitcast.5) | data formatting | bytes 1572864
  69.5 0.7 %copy.15 = f32[1,128,768]{2,1,0:T(8,128)} copy(f32[1,128,768]{2,1,0:T(8,128)S(1)} %bitcast.6) | data formatting | bytes 786432
  70.3 0.6 copy.16

commit v6 on v5

--- a/solution.py
+++ b/solution.py
@@ -111,7 +111,7 @@
     owned = [pltpu.make_async_copy(head, heads.at[mine], local_sem.at[1])]
     own_columns = [
         pltpu.make_async_copy(
-            teach.at[:, :, columns_of(x, b)], arrived.at[x, :, :, pl.ds(b * 256, 256)], local_sem.at[2]
+            teach.at[:, columns_of(x, b)], arrived.at[x, :, pl.ds(b * 256, 256)], local_sem.at[2]
         )
         for b in range(4)
     ]
@@ -142,7 +142,7 @@
     for k in (1, 3, 2):
         for b in range(4):
             columns = columns_of((x + k) % 4, b)
-            send(teach.at[:, :, columns], arrived.at[x, :, :, pl.ds(b * 256, 256)], device(dx=k), slices)
+            send(teach.at[:, columns], arrived.at[x, :, pl.ds(b * 256, 256)], device(dx=k), slices)
     head_z = group(head)
     send(head, heads.at[mine], device(dz=4), head_z)
     head_y = group(heads.at[pl.ds(0, 6)])
@@ -179,7 +179,7 @@
     arrive(slices)
     for copy in owned:
         copy.wait()
-    own = dot(permutation(128, image_order), arrived[...].astype(F32).reshape(128, SLICE).astype(BF16), ((1,), (0,)))
+    own = dot(permutation(128, image_order), arrived[...].reshape(128, SLICE), ((1,), (0,)))
     target = (near_target, far_target)
     near_target[0, :, core] = own.astype(BF16).reshape(8, 16, SLICE)
     places = {0: (0, 0), -1: (0, 1), 1: (0, 2), -2: (0, 3), 4: (1, 0), -4: (1, 0), 3: (1, 1), -3: (1, 2), 2: (1, 3)}
@@ -515,7 +515,7 @@
     smem = pl.BlockSpec(memory_space=pltpu.SMEM)
     anywhere = pl.BlockSpec(memory_space=pl.ANY)
     operands = (
-        teacher_feats, student_feats.reshape(2 * MAIN, WIDTH), norm_gain, head_weight.reshape(128, WIDTH),
+        student_feats.reshape(2 * MAIN, WIDTH), norm_gain, head_weight.reshape(128, WIDTH),
         slot_image.transpose(0, 1, 3, 2), slot_count,
     )
     loss, gain_grad, sgrad, hgrad = pl.pallas_call(
@@ -529,7 +529,7 @@
         in_specs=[anywhere] * 6,
         out_specs=(smem, vmem, vmem, vmem),
         scratch_shapes=[
-            pltpu.VMEM((4, 8, 4, SLICE), BF16),
+            pltpu.VMEM((4, 32, SLICE), BF16),
             pltpu.VMEM((4, 8, 2, 16, SLICE), BF16),
             pltpu.VMEM((4, 8, 2, 16, SLICE), BF16),
             pltpu.VMEM((8, 128, WIDTH), BF16),
@@ -574,7 +574,7 @@
             collective_id=0, has_side_effects=True, vmem_limit_bytes=44 << 20
         ),
         name="head_step",
-    )(*[pltpu.with_memory_space_constraint(operand, pltpu.HBM) for operand in operands])
+    )(teacher_feats.reshape(32, FEAT), *[pltpu.with_memory_space_constraint(operand, pltpu.HBM) for operand in operands])
     return (
         loss,
         sgrad.reshape(student_feats.shape),

time: 72.9 us -> 74.1 us (1.016)
  local copies, waits for them, and re-layouts: 2.2 us -> 3.22 us
    reshape x0 -> x1, local copies, waits for them, and re-layouts: none -> 1.01 us  [shards(): teacher_feats.reshape(32, FEAT)]
where the time goes in v6:
time: 74.1 us; the launch traced here: 73.5 us
  Pallas kernels  67.9 us (92%)
  local copies, waits for them, and re-layouts  3.22 us (4%)
  between operations  2.33 us (3%)
    pallas_call x1, Pallas kernels, shards(): pl.pallas_call(kernel, out_shape=(jax.ShapeDtypeStruct((1,), F32), pltpu....  67.9 us
    unnamed x3, local copies, waits for them, and re-layouts  2.2 us

profile of v6, /device:TPU:1, one launch (start us, length us, event | category | flops | bytes accessed | tf_op | source)
XLA Modules:
  0.0 73.5 jit_solution(18209523732506381995)
XLA Ops:
  0.6 1.0 %reshape.23.teach = bf16[32,4096]{1,0:T(8,128)(2,1)S(1)} reshape(bf16[8,4,4096]{2,1,0:T(4,128)(2,1)} %param.6) | data formatting | bytes 524288 | tf_op jit(solution)/shard_map/reshape | solution.py:577
  1.6 67.9 %head_step.1 = (f32[1]{0:T(128)}, f32[1,768]{1,0:T(1,128)S(1)}, bf16[512,768]{1,0:T(8,128)(2,1)S(1)}, f32[128,768]{1,0:T(8,128)S(1)}) custom-call(bf16[32,4096]{1,0:T(8,128)(2,1)S(1)} %reshape.23.teach, bf16[512,768]{1,0:T(8,128)(2,1)} %bitcast.7, f32[1,768]{1,0:T(1,128)} %gain_h.1, bf16[128,768]{1,0:T(8,128)(2,1)} %bitcast.8, s32[8,1,2,8]{3,2,1,0:T(2,128)} %bitcast.9, ...), custom_call_target="tpu_custom_call" | custom-call | tf_op jit(solution)/shard_map/head_step/pallas_call | solution.py:521
  69.6 0.9 %copy.14 = bf16[1,1,1,2,256,768]{5,4,3,2,1,0:T(8,128)(2,1)} copy(bf16[1,1,1,2,256,768]{5,4,3,2,1,0:T(8,128)(2,1)S(1)} %bitcast.5) | data formatting | bytes 1572864
  70.4 0.7 %copy.15 = f32[1,128,768]{2,1,0:T(8,128)} copy(f32[1,128,768]{2,1,0:T(8,128)S(1)} %bitcast.6) | data formatting | bytes 786432
  71.2 0.6 copy.16
